TPU v7x, 256 devices: a whole 4x4x8 slice. The times are simulated.
256 devices in a mesh: region: 16 (over x, y), replica: 8 (over z), tensor: 2 (over core).
Axes of the slice: x: 4, y: 4, z: 8, core: 2. Of those that a mesh axis runs over, the one named last changes fastest.
Arguments:
- gradient: bfloat16 [8, 16, 8192, 256], P('replica', 'region', None, 'tensor'), parts along dimension 3, may hold values from -6 to 6
- feedback: float32 [8, 16, 8192, 256], P('replica', 'region', None, 'tensor'), parts along dimension 3, may hold values from -4 to 4
- picked: int32 [8, 16, 16, 128], P('replica', 'region', None, 'tensor'), parts along dimension 3, may hold values from 0 to 511, as said below
- counts: int32 [8, 16, 32], P('replica', 'region', 'tensor'), parts along dimension 2, may hold values from 0 to 64, as said below
- weights: float32 [8192, 256], P(('region', 'replica'), 'tensor'), parts along dimension 1, may hold values from -6 to 6
- moment: float32 [8192, 256], P(('region', 'replica'), 'tensor'), parts along dimension 1, may hold values from -3 to 3
- second: float32 [8192, 256], P(('region', 'replica'), 'tensor'), parts along dimension 1, may hold values from 0.01 to 1
Outputs:
- new_weights: float32 [8192, 256], P(('region', 'replica'), 'tensor'), parts along dimension 1
- new_moment: float32 [8192, 256], P(('region', 'replica'), 'tensor'), parts along dimension 1
- new_second: float32 [8192, 256], P(('region', 'replica'), 'tensor'), parts along dimension 1
- new_feedback: float32 [8, 16, 8192, 256], P('replica', 'region', None, 'tensor'), parts along dimension 3
There are 2 independent parts, one for each index of `tensor`. A program takes and returns all parts, laid end to end along the dimension named above; each array names one. Nothing has to cross between parts.
Inputs may be any that keep to these rules, and one draw needn't show every extreme that they name: `picked`: for each worker and owner, 64 distinct block numbers within the owner's region; slots at or past the count are ignored. `counts`: in every replica some owner gets 64 live slots from every worker of the region.
All inputs are finite; a program needn't handle non-finite values.
Results may differ from a plain program's by a relative error of at most 0.0003.
Values sent between devices are 32-bit elements; how exact they have to be, the bound alone decides.
No kernel may reach another device: no remote copies, remote signals or barrier semaphores. Data moves between devices by JAX's collectives and lax.ppermute only.
A program may use at most 64 MiB of HBM per device.

v0:
```python
import jax
import jax.numpy as jnp
from jax import lax
from jax.sharding import PartitionSpec as P


def swapped(value, axis, distance):
    mask = 2**distance
    pairs = [(source, source ^ mask) for source in range(lax.axis_size(axis))]
    return lax.ppermute(value, axis, pairs)


def body(gradient, feedback, picked, counts, weights, moment, second):
    owners = lax.axis_size("region")
    compensated = gradient[0, 0].astype(jnp.float32) + feedback[0, 0]
    width = compensated.shape[1]
    own_rows = weights.shape[0]
    reg_rows = own_rows * lax.axis_size("replica")
    block_ids = picked[0, 0]
    slot_count = block_ids.shape[1]
    live = lax.broadcasted_iota(jnp.int32, (owners, slot_count), 1) < counts[0, 0][:, None]
    keep = live.astype(jnp.float32)
    offsets = lax.broadcasted_iota(jnp.int32, (owners, slot_count), 0) * reg_rows
    rows = (block_ids + offsets).reshape(-1)
    tiles = compensated[rows].reshape(owners, slot_count, width) * keep[:, :, None]
    flags = jnp.zeros((compensated.shape[0],), jnp.float32).at[rows].max(keep.reshape(-1))
    new_feedback = (compensated * (1.0 - flags)[:, None])[None, None]
    got_tiles, got_ids = (
        lax.all_to_all(tiles, "region", split_axis=0, concat_axis=0, tiled=True),
        lax.all_to_all(block_ids, "region", split_axis=0, concat_axis=0, tiled=True),
    )
    region_sum = (
        jnp.zeros((reg_rows, width), jnp.float32)
        .at[got_ids.reshape(-1)]
        .add(got_tiles.reshape(-1, width))
    )
    levels = lax.axis_size("replica").bit_length() - 1
    for bit in range(levels):
        region_sum = region_sum + swapped(region_sum, "replica", bit)
    start = lax.axis_index("replica") * own_rows
    total = lax.dynamic_slice_in_dim(region_sum, start, own_rows, 0)
    new_moment = 0.9 * moment + 0.1 * total
    new_second = 0.95 * second + 0.05 * total * total
    new_weights = weights - 0.02 * (new_moment / (jnp.sqrt(new_second) + 1e-08) + 0.1 * weights)
    return (new_weights, new_moment, new_second, new_feedback)


def solution(mesh):
    placed = (
        P("replica", "region", None, "tensor"),
        P("replica", "region", None, "tensor"),
        P("replica", "region", None, "tensor"),
        P("replica", "region", "tensor"),
        P(("region", "replica"), "tensor"),
        P(("region", "replica"), "tensor"),
        P(("region", "replica"), "tensor"),
    )
    return jax.shard_map(
        body,
        mesh=mesh,
        in_specs=placed,
        out_specs=(
            P(("region", "replica"), "tensor"),
            P(("region", "replica"), "tensor"),
            P(("region", "replica"), "tensor"),
            P("replica", "region", None, "tensor"),
        ),
        check_vma=False,
    )
```

profile of v0, /device:TPU:8, one launch (start us, length us, event | category | flops | bytes accessed | tf_op | source)
XLA Modules:
  0.0 90.6 jit_solution(8623389303837704847)
XLA Ops:
  0.6 7.4 %all-to-all-start = ((s32[16,1,64]{2,1,0:T(1,128)}), s32[16,1,64]{2,1,0:T(1,128)S(1)}, u32[]{:S(2)}, u32[]{:S(2)}) async-start(s32[16,1,64]{2,1,0:T(1,128)} %bitcast.12), calls=%async_computation | async-start | bytes 16384 | tf_op jit(solution)/shard_map/all_to_all | solution.py:30
  8.0 0.8 squeeze.2
  8.8 0.1 iota.18
  8.9 0.1 iota.19
  9.0 0.7 fusion.7
  9.7 0.1 reshape.139
  9.8 7.6 %scatter_custom_fusion.1 = f32[8192]{0:T(1024)S(1)} fusion(s32[1024]{0:T(1024)S(1)} %bitcast.14, f32[1024]{0:T(1024)S(1)} %reshape.139, f32[]{:T(128)} %constant.15.clone.1), kind=kCustom, calls=%fused_computation.16 | custom fusion | flops 1024 | bytes 32772 | tf_op jit(solution)/shard_map/scatter-max | solution.py:26
  17.5 5.7 %fusion = (f32[1,1,8192,128]{3,2,1,0:T(8,128)}, f32[8192,128]{1,0:T(8,128)}) fusion(f32[1,1,8192,128]{3,2,1,0:T(8,128)} %param.8, bf16[1,1,8192,128]{3,2,1,0:T(8,128)(2,1)} %param.7, f32[8192]{0:T(1024)S(1)} %broadcast_subtract_fusion), kind=kLoop, calls=%fused_computation.4 | loop fusion | flops 3145728 | bytes 14712832 | tf_op jit(solution)/shard_map/mul | solution.py:27
  23.2 0.0 copy-start
  23.2 0.0 copy-start.1
  23.2 0.0 copy-start.2
  23.2 5.0 %gather_fusion = f32[1024,128]{1,0:T(8,128)S(1)} fusion(f32[8192,128]{1,0:T(8,128)} %get-tuple-element.8, s32[1024]{0:T(1024)S(1)} %broadcast_clamp_fusion), kind=kCustom, calls=%fused_computation | custom fusion | bytes 1052672 | tf_op jit(solution)/shard_map/gather | solution.py:25
  28.3 1.0 %broadcast_multiply_fusion = f32[16,64,128]{2,1,0:T(8,128)} fusion(f32[16,64,128]{2,1,0:T(8,128)S(1)} %bitcast.10, f32[16,64]{1,0:T(8,128)S(1)} %fusion.7), kind=kLoop, calls=%fused_computation.6 | loop fusion | flops 131072 | bytes 1052672 | tf_op jit(solution)/shard_map/mul | solution.py:25
  29.2 0.0 all-to-all-done
  29.2 7.2 %all-to-all-start.1 = ((f32[16,64,128]{2,1,0:T(8,128)}), f32[16,64,128]{2,1,0:T(8,128)S(1)}, u32[]{:S(2)}, u32[]{:S(2)}) async-start(f32[16,64,128]{2,1,0:T(8,128)} %broadcast_multiply_fusion), calls=%async_computation.1 | async-start | bytes 1048576 | tf_op jit(solution)/shard_map/all_to_all | solution.py:29
  36.5 0.5 broadcast.72
  37.0 0.7 reduce.3
  37.7 0.1 reshape.115
  37.8 8.3 %all-to-all-done.1 = f32[16,64,128]{2,1,0:T(8,128)S(1)} async-done(((f32[16,64,128]{2,1,0:T(8,128)}), f32[16,64,128]{2,1,0:T(8,128)S(1)}, u32[]{:S(2)}, u32[]{:S(2)}) %all-to-all-start.1) | async-done | bytes 524320 | tf_op jit(solution)/shard_map/all_to_all | solution.py:29
  46.0 6.1 %scatter_custom_fusion = f32[512,128]{1,0:T(8,128)S(1)} fusion(s32[1024]{0:T(1024)S(1)} %bitcast.15, f32[1024,128]{1,0:T(8,128)S(1)} %bitcast.11, f32[]{:T(128)} %constant.15.clone.1), kind=kCustom, calls=%fused_computation.7 | custom fusion | flops 131072 | bytes 262148 | tf_op jit(solution)/shard_map/scatter-add | solution.py:35
  52.1 2.0 %collective-permute-start = (f32[512,128]{1,0:T(8,128)S(1)}, f32[512,128]{1,0:T(8,128)S(1)}, u32[]{:S(2)}, u32[]{:S(2)}) collective-permute-start(f32[512,128]{1,0:T(8,128)S(1)} %scatter_custom_fusion), channel_id=1, source_target_pairs={{0,2},{2,0},{4,6},{6,4},{8,10},{10,8},{12,14},{14,12},{1,3},{3,1},... | collective-permute-start | bytes 786440 | tf_op jit(solution)/shard_map/ppermute | solution.py:10
  54.1 4.5 %collective-permute-done = f32[512,128]{1,0:T(8,128)S(1)} collective-permute-done((f32[512,128]{1,0:T(8,128)S(1)}, f32[512,128]{1,0:T(8,128)S(1)}, u32[]{:S(2)}, u32[]{:S(2)}) %collective-permute-start) | collective-permute-done | bytes 262176 | tf_op jit(solution)/shard_map/ppermute | solution.py:10
  58.6 4.6 %collective-permute-start.1 = (f32[512,128]{1,0:T(8,128)S(1)}, f32[512,128]{1,0:T(8,128)S(1)}, u32[]{:S(2)}, u32[]{:S(2)}) collective-permute-start(f32[512,128]{1,0:T(8,128)S(1)} %add.77), channel_id=1, source_target_pairs={{0,4},{2,6},{4,0},{6,2},{8,12},{10,14},{12,8},{14,10},{1,5},{3,7},... | collective-permute-start | bytes 786440 | tf_op jit(solution)/shard_map/ppermute | solution.py:10
  63.2 7.2 %collective-permute-done.1 = f32[512,128]{1,0:T(8,128)S(1)} collective-permute-done((f32[512,128]{1,0:T(8,128)S(1)}, f32[512,128]{1,0:T(8,128)S(1)}, u32[]{:S(2)}, u32[]{:S(2)}) %collective-permute-start.1) | collective-permute-done | bytes 262176 | tf_op jit(solution)/shard_map/ppermute | solution.py:10
  70.4 12.4 %collective-permute-start.2 = (f32[512,128]{1,0:T(8,128)S(1)}, f32[512,128]{1,0:T(8,128)S(1)}, u32[]{:S(2)}, u32[]{:S(2)}) collective-permute-start(f32[512,128]{1,0:T(8,128)S(1)} %add.78), channel_id=1, source_target_pairs={{0,8},{2,10},{4,12},{6,14},{8,0},{10,2},{12,4},{14,6},{1,9},{3,11}... | collective-permute-start | bytes 786440 | tf_op jit(solution)/shard_map/ppermute | solution.py:10
  82.8 7.2 %collective-permute-done.2 = f32[512,128]{1,0:T(8,128)S(1)} collective-permute-done((f32[512,128]{1,0:T(8,128)S(1)}, f32[512,128]{1,0:T(8,128)S(1)}, u32[]{:S(2)}, u32[]{:S(2)}) %collective-permute-start.2) | collective-permute-done | bytes 262176 | tf_op jit(solution)/shard_map/ppermute | solution.py:10
  90.0 0.0 copy-done
  90.0 0.0 copy-done.1
  90.0 0.0 copy-done.2
  90.0 0.7 multiply_subtract_fusion
  (7 shorter events, 0.1 us)
Async XLA Ops:
  0.6 28.6 %all-to-all-start = ((s32[16,1,64]{2,1,0:T(1,128)}), s32[16,1,64]{2,1,0:T(1,128)S(1)}, u32[]{:S(2)}, u32[]{:S(2)}) async-start(s32[16,1,64]{2,1,0:T(1,128)} %bitcast.12), calls=%async_computation | async-start | bytes 16384 | tf_op jit(solution)/shard_map/all_to_all | solution.py:30
  23.2 66.8 %copy-start = (f32[64,128]{1,0:T(8,128)S(1)}, f32[64,128]{1,0:T(8,128)}, u32[]{:S(2)}) copy-start(f32[64,128]{1,0:T(8,128)} %param.11) | copy-start | bytes 98308
  23.2 66.8 %copy-start.1 = (f32[64,128]{1,0:T(8,128)S(1)}, f32[64,128]{1,0:T(8,128)}, u32[]{:S(2)}) copy-start(f32[64,128]{1,0:T(8,128)} %param.13) | copy-start | bytes 98308
  23.2 66.8 %copy-start.2 = (f32[64,128]{1,0:T(8,128)S(1)}, f32[64,128]{1,0:T(8,128)}, u32[]{:S(2)}) copy-start(f32[64,128]{1,0:T(8,128)} %param.12) | copy-start | bytes 98308
  29.2 16.8 %all-to-all-start.1 = ((f32[16,64,128]{2,1,0:T(8,128)}), f32[16,64,128]{2,1,0:T(8,128)S(1)}, u32[]{:S(2)}, u32[]{:S(2)}) async-start(f32[16,64,128]{2,1,0:T(8,128)} %broadcast_multiply_fusion), calls=%async_computation.1 | async-start | bytes 1048576 | tf_op jit(solution)/shard_map/all_to_all | solution.py:29
  52.1 6.5 %collective-permute-start = (f32[512,128]{1,0:T(8,128)S(1)}, f32[512,128]{1,0:T(8,128)S(1)}, u32[]{:S(2)}, u32[]{:S(2)}) collective-permute-start(f32[512,128]{1,0:T(8,128)S(1)} %scatter_custom_fusion), channel_id=1, source_target_pairs={{0,2},{2,0},{4,6},{6,4},{8,10},{10,8},{12,14},{14,12},{1,3},{3,1},... | collective-permute-start | bytes 786440 | tf_op jit(solution)/shard_map/ppermute | solution.py:10
  58.6 11.7 %collective-permute-start.1 = (f32[512,128]{1,0:T(8,128)S(1)}, f32[512,128]{1,0:T(8,128)S(1)}, u32[]{:S(2)}, u32[]{:S(2)}) collective-permute-start(f32[512,128]{1,0:T(8,128)S(1)} %add.77), channel_id=1, source_target_pairs={{0,4},{2,6},{4,0},{6,2},{8,12},{10,14},{12,8},{14,10},{1,5},{3,7},... | collective-permute-start | bytes 786440 | tf_op jit(solution)/shard_map/ppermute | solution.py:10
  70.4 19.6 %collective-permute-start.2 = (f32[512,128]{1,0:T(8,128)S(1)}, f32[512,128]{1,0:T(8,128)S(1)}, u32[]{:S(2)}, u32[]{:S(2)}) collective-permute-start(f32[512,128]{1,0:T(8,128)S(1)} %add.78), channel_id=1, source_target_pairs={{0,8},{2,10},{4,12},{6,14},{8,0},{10,2},{12,4},{14,6},{1,9},{3,11}... | collective-permute-start | bytes 786440 | tf_op jit(solution)/shard_map/ppermute | solution.py:10
where the time goes:
time: 91 us; the launch traced here: 90.6 us
  starting transfers between devices  33.6 us (37%)
  waiting for transfers between devices  27.1 us (30%)
  other arithmetic  22.6 us (25%)
  local copies, waits for them, and re-layouts  6.65 us (7%)
    ppermute x3, starting transfers between devices, swapped(): return lax.ppermute(value, axis, pairs)  19 us
    ppermute x3, waiting for transfers between devices, swapped(): return lax.ppermute(value, axis, pairs)  18.8 us
    all_to_all x1, waiting for transfers between devices, body(): lax.all_to_all(tiles, 'region', split_axis=0, concat_axis=0, tiled=True)  8.29 us
    another operation x1, other arithmetic, body(): jnp.zeros((compensated.shape[0],), jnp.float32).at[rows]  7.64 us
    all_to_all x1, starting transfers between devices, body(): lax.all_to_all(block_ids, 'region', split_axis=0, concat_axis=0, tiled=True)  7.4 us
    all_to_all x1, starting transfers between devices, body(): lax.all_to_all(tiles, 'region', split_axis=0, concat_axis=0, tiled=True)  7.23 us
    scatter-add x1, other arithmetic, body(): region_sum = jnp.zeros((reg_rows, width), jnp.float32).at[got_ids.reshape...  6.08 us
    mul x1, other arithmetic, body(): new_feedback = (compensated * (1.0 - flags)[:, None])[None, None]  5.74 us
  transfers between devices with their start and end apart: 5, of which 4 were waited for; matrix products, arithmetic and copies ran while one was open for 25% of the time, Pallas kernels for 0%

commit v1 on v0

v1 whole, which is shorter than its diff:
```python
import functools

import jax
import jax.numpy as jnp
from jax import lax
from jax.experimental import pallas as pl
from jax.experimental.pallas import tpu as pltpu
from jax.sharding import PartitionSpec as P


def split(value):
    high = value.astype(jnp.bfloat16)
    low = (value - high.astype(jnp.float32)).astype(jnp.bfloat16)
    return jnp.concatenate([high, low], axis=1)


def one_hot(rows, ids):
    row = lax.broadcasted_iota(jnp.int32, (rows, ids.shape[1]), 0)
    return jnp.where(row == ids, 1.0, 0.0).astype(jnp.bfloat16)


def pack_kernel(counts, picked, gradient, feedback, tiles, new_feedback):
    owner = pl.program_id(0)
    slots = picked.shape[-1]
    rows, width = gradient.shape[2:]
    compensated = gradient[0, 0].astype(jnp.float32) + feedback[0, 0]
    slot = lax.broadcasted_iota(jnp.int32, (1, slots), 1)
    ids = jnp.where(slot < counts[0, 0, owner], picked[0, 0, pl.ds(owner, 1), :], -1)
    hot = one_hot(rows, ids)
    named = jnp.dot(hot, jnp.ones((slots, width), jnp.bfloat16), preferred_element_type=jnp.float32)
    new_feedback[0, 0] = jnp.where(named > 0.0, 0.0, compensated)
    halves = lax.dot_general(hot, split(compensated), (((0,), (0,)), ((), ())), preferred_element_type=jnp.float32)
    tiles[0, :slots, :] = halves[:, :width] + halves[:, width:]
    sent = ids.astype(jnp.float32)
    tiles[0, slots:, :] = jnp.broadcast_to(jnp.concatenate([sent, sent], axis=1), (tiles.shape[1] - slots, width))


def pack(counts, picked, gradient, feedback):
    owners, slots = picked.shape[2:]
    blocks, width = gradient.shape[2:]
    rows = blocks // owners
    whole = pl.BlockSpec((1, 1, rows, width), lambda o: (0, 0, o, 0))
    return pl.pallas_call(
        pack_kernel,
        grid=(owners,),
        in_specs=[
            pl.BlockSpec(memory_space=pltpu.SMEM),
            pl.BlockSpec((1, 1, owners, slots), lambda o: (0, 0, 0, 0)),
            whole,
            whole,
        ],
        out_specs=[pl.BlockSpec((1, slots + 8, width), lambda o: (o, 0, 0)), whole],
        out_shape=[
            jax.ShapeDtypeStruct((owners, slots + 8, width), jnp.float32),
            jax.ShapeDtypeStruct(feedback.shape, jnp.float32),
        ],
        compiler_params=pltpu.CompilerParams(vmem_limit_bytes=48 * 2**20),
        name="pack",
    )(counts, picked, gradient, feedback)


def gather_sum_kernel(slots, rows, got, kept, sent, hot, parts):
    me = lax.axis_index("replica")
    sources, _, width = got.shape
    lane = lax.broadcasted_iota(jnp.int32, (1, 2 * slots), 1)
    for pair in range(sources // 2):
        first, second = 2 * pair, 2 * pair + 1
        ids = jnp.where(lane < slots, got[first, slots : slots + 1, :], got[second, slots : slots + 1, :])
        ids = ids.astype(jnp.int32)
        far = (ids >> 6) ^ me
        place = jnp.where(ids < 0, -1, ((far & 1) << 8) | ((far >> 1) << 6) | (ids & 63))
        hot[:, pair * 2 * slots : (pair + 1) * 2 * slots] = one_hot(rows, place)
        for source in (first, second):
            parts[source * slots : (source + 1) * slots, :] = split(got[source, :slots, :])
    halves = jnp.dot(hot[...], parts[...], preferred_element_type=jnp.float32)
    total = halves[:, :width] + halves[:, width:]
    kept[...] = total[: rows // 2]
    sent[...] = total[rows // 2 :]


def gather_sum(got, rows):
    sources, _, width = got.shape
    slots = width // 2
    half = jax.ShapeDtypeStruct((rows // 2, width), jnp.float32)
    return pl.pallas_call(
        functools.partial(gather_sum_kernel, slots, rows),
        in_specs=[pl.BlockSpec(memory_space=pltpu.VMEM)],
        out_specs=[pl.BlockSpec(memory_space=pltpu.VMEM)] * 2,
        out_shape=[half, half],
        scratch_shapes=[
            pltpu.VMEM((rows, sources * slots), jnp.bfloat16),
            pltpu.VMEM((sources * slots, 2 * width), jnp.bfloat16),
        ],
        compiler_params=pltpu.CompilerParams(vmem_limit_bytes=48 * 2**20),
        name="gather_sum",
    )(got)


def swapped(value, mask):
    return lax.ppermute(value, "replica", [(source, source ^ mask) for source in range(lax.axis_size("replica"))])


def body(gradient, feedback, picked, counts, weights, moment, second):
    own_rows = weights.shape[0]
    reg_rows = own_rows * lax.axis_size("replica")
    tiles, new_feedback = pack(counts, picked, gradient, feedback)
    got = lax.all_to_all(tiles, "region", split_axis=0, concat_axis=0, tiled=True)
    kept, sent = gather_sum(got, reg_rows)
    part = (kept + swapped(sent, 1)).reshape(4, own_rows, kept.shape[1])
    far = [swapped(part[pair], 2 * pair) for pair in (2, 1, 3)]
    total = part[0] + far[0] + far[1] + far[2]
    new_moment = 0.9 * moment + 0.1 * total
    new_second = 0.95 * second + 0.05 * total * total
    new_weights = weights - 0.02 * (new_moment / (jnp.sqrt(new_second) + 1e-08) + 0.1 * weights)
    return (new_weights, new_moment, new_second, new_feedback)


def solution(mesh):
    placed = (
        P("replica", "region", None, "tensor"),
        P("replica", "region", None, "tensor"),
        P("replica", "region", None, "tensor"),
        P("replica", "region", "tensor"),
        P(("region", "replica"), "tensor"),
        P(("region", "replica"), "tensor"),
        P(("region", "replica"), "tensor"),
    )
    return jax.shard_map(
        body,
        mesh=mesh,
        in_specs=placed,
        out_specs=(
            P(("region", "replica"), "tensor"),
            P(("region", "replica"), "tensor"),
            P(("region", "replica"), "tensor"),
            P("replica", "region", None, "tensor"),
        ),
        check_vma=False,
    )
```

time: 91 us -> 53.6 us (0.59)
  the two profiles are of different devices: /device:TPU:8 before, /device:TPU:32 now
where the time goes in v1:
time: 53.6 us; the launch traced here: 53.2 us
  blocking collectives  19 us (35%)
  Pallas kernels  12 us (22%)
  waiting for transfers between devices  9.06 us (17%)
  starting transfers between devices  8.75 us (16%)
  local copies, waits for them, and re-layouts  2.95 us (6%)
  other arithmetic  0.68 us (1%)
  between operations  0.67 us (1%)
    all_to_all x1, blocking collectives, body(): lax.all_to_all(tiles, 'region', split_axis=0, concat_axis=0, tiled=True)  19 us
    pallas_call x1, Pallas kernels, pack(): pl.pallas_call(pack_kernel, grid=(owners,), in_specs=[pl.BlockSpec(memory...  11.4 us
    ppermute x4, waiting for transfers between devices, swapped(): lax.ppermute(value, 'replica', [(source, source ^ mask) for source in ran...  9.06 us
    ppermute x4, starting transfers between devices, swapped(): lax.ppermute(value, 'replica', [(source, source ^ mask) for source in ran...  8.75 us
    unnamed x12, local copies, waits for them, and re-layouts  2.95 us
  transfers between devices with their start and end apart: 4, of which 3 were waited for; matrix products, arithmetic and copies ran while one was open for 0% of the time, Pallas kernels for 0%

profile of v1, /device:TPU:32, one launch (start us, length us, event | category | flops | bytes accessed | tf_op | source)
XLA Modules:
  0.0 53.2 jit_solution(13549296211575469236)
XLA Ops:
  0.6 0.0 copy-start
  0.6 1.6 %copy-done = bf16[1,1,8192,128]{3,2,1,0:T(8,128)(2,1)S(1)} copy-done((bf16[1,1,8192,128]{3,2,1,0:T(8,128)(2,1)S(1)}, bf16[1,1,8192,128]{3,2,1,0:T(8,128)(2,1)}, u32[]{:S(2)}) %copy-start) | copy-done | bytes 2097176
  2.2 0.0 copy-start.1
  2.2 0.7 %copy-done.1 = s32[1,1,16,64]{3,2,1,0:T(8,128)S(1)} copy-done((s32[1,1,16,64]{3,2,1,0:T(8,128)S(1)}, s32[1,1,16,64]{3,2,1,0:T(8,128)}, u32[]{:S(2)}) %copy-start.1) | copy-done | bytes 4120
  2.9 0.0 copy-start.2
  2.9 0.7 %copy-done.2 = s32[1,1,16]{2,1,0:T(1,128)S(1)} copy-done((s32[1,1,16]{2,1,0:T(1,128)S(1)}, s32[1,1,16]{2,1,0:T(1,128)}, u32[]{:S(2)}) %copy-start.2) | copy-done | bytes 88
  3.6 0.0 copy-start.3
  3.6 0.0 copy-start.4
  3.6 0.0 copy-start.5
  3.6 11.4 %pack.1 = (f32[16,72,128]{2,1,0:T(8,128)S(1)}, f32[1,1,8192,128]{3,2,1,0:T(8,128)}) custom-call(s32[1,1,16]{2,1,0:T(1,128)S(1)} %copy-done.2, s32[1,1,16,64]{3,2,1,0:T(8,128)S(1)} %copy-done.1, bf16[1,1,8192,128]{3,2,1,0:T(8,128)(2,1)S(1)} %copy-done, f32[1,1,8192,128]{3,2,1,0:T(8,128)} %feedback.1), custom_call_target="tpu_custom_call" | custom-call | tf_op jit(solution)/shard_map/pack/pallas_call | solution.py:43
  15.0 19.0 %all_to_all.5.got = f32[16,72,128]{2,1,0:T(8,128)S(1)} all-to-all(f32[16,72,128]{2,1,0:T(8,128)S(1)} %get-tuple-element.8), channel_id=1, replica_groups=mesh['region'=16,'replica'=8,'tensor'=2] {'region'}, dimensions={0} | all-to-all | bytes 1179648 | tf_op jit(solution)/shard_map/all_to_all | solution.py:107
  34.1 0.6 %gather_sum.1 = (f32[256,128]{1,0:T(8,128)S(1)}, f32[256,128]{1,0:T(8,128)S(1)}) custom-call(f32[16,72,128]{2,1,0:T(8,128)S(1)} %all_to_all.5.got), custom_call_target="tpu_custom_call" | custom-call | tf_op jit(solution)/shard_map/gather_sum/pallas_call | solution.py:85
  34.7 0.2 collective-permute-start
  34.9 4.9 %collective-permute-done = f32[256,128]{1,0:T(8,128)S(1)} collective-permute-done((f32[256,128]{1,0:T(8,128)S(1)}, f32[256,128]{1,0:T(8,128)S(1)}, u32[]{:S(2)}, u32[]{:S(2)}) %collective-permute-start) | collective-permute-done | bytes 131104 | tf_op jit(solution)/shard_map/ppermute | solution.py:100
  39.8 6.7 %collective-permute-start.1 = (f32[64,128]{1,0:T(8,128)S(1)}, f32[64,128]{1,0:T(8,128)S(1)}, u32[]{:S(2)}, u32[]{:S(2)}) collective-permute-start(f32[64,128]{1,0:T(8,128)S(1)} %get-tuple-element.15), channel_id=1, source_target_pairs={{0,8},{2,10},{4,12},{6,14},{8,0},{10,2},{12,4},{14,6},{1,9},{3,11}... | collective-permute-start | bytes 98312 | tf_op jit(solution)/shard_map/ppermute | solution.py:100
  46.5 0.2 collective-permute-start.3
  46.7 1.6 %collective-permute-start.2 = (f32[64,128]{1,0:T(8,128)S(1)}, f32[64,128]{1,0:T(8,128)S(1)}, u32[]{:S(2)}, u32[]{:S(2)}) collective-permute-start(f32[64,128]{1,0:T(8,128)S(1)} %get-tuple-element.17), channel_id=1, source_target_pairs={{0,4},{2,6},{4,0},{6,2},{8,12},{10,14},{12,8},{14,10},{1,5},{3,7},... | collective-permute-start | bytes 98312 | tf_op jit(solution)/shard_map/ppermute | solution.py:100
  48.3 0.1 collective-permute-done.1
  48.4 4.1 %collective-permute-done.3 = f32[64,128]{1,0:T(8,128)S(1)} collective-permute-done((f32[64,128]{1,0:T(8,128)S(1)}, f32[64,128]{1,0:T(8,128)S(1)}, u32[]{:S(2)}, u32[]{:S(2)}) %collective-permute-start.3) | collective-permute-done | bytes 32800 | tf_op jit(solution)/shard_map/ppermute | solution.py:100
  52.5 0.0 collective-permute-done.2
  52.5 0.0 copy-done.3
  52.5 0.0 copy-done.4
  52.5 0.0 copy-done.5
  52.5 0.7 %multiply_subtract_fusion = (f32[64,128]{1,0:T(8,128)}, f32[64,128]{1,0:T(8,128)}, f32[64,128]{1,0:T(8,128)}) fusion(f32[64,128]{1,0:T(8,128)S(1)} %copy-done.3, f32[64,128]{1,0:T(8,128)S(1)} %copy-done.4, f32[64,128]{1,0:T(8,128)S(1)} %copy-done.5, f32[64,128]{1,0:T(8,128)S(1)} %collective-permute-done.3, f32[64,128]{1,0:T(8,128)S(1)} %collective-permute-done.2, ...), kind=kLoop, calls=%fused_computation.5 | loop fusion | flops 131072 | bytes 327680 | tf_op jit(solution)/shard_map/sub | solution.py:114
  (2 shorter events, 0.0 us)
Async XLA Ops:
  0.6 1.6 %copy-start = (bf16[1,1,8192,128]{3,2,1,0:T(8,128)(2,1)S(1)}, bf16[1,1,8192,128]{3,2,1,0:T(8,128)(2,1)}, u32[]{:S(2)}) copy-start(bf16[1,1,8192,128]{3,2,1,0:T(8,128)(2,1)} %gradient.1) | copy-start | bytes 6291460
  2.2 0.7 %copy-start.1 = (s32[1,1,16,64]{3,2,1,0:T(8,128)S(1)}, s32[1,1,16,64]{3,2,1,0:T(8,128)}, u32[]{:S(2)}) copy-start(s32[1,1,16,64]{3,2,1,0:T(8,128)} %picked.1) | copy-start | bytes 12292
  2.9 0.7 %copy-start.2 = (s32[1,1,16]{2,1,0:T(1,128)S(1)}, s32[1,1,16]{2,1,0:T(1,128)}, u32[]{:S(2)}) copy-start(s32[1,1,16]{2,1,0:T(1,128)} %counts.1) | copy-start | bytes 196
  3.6 48.9 %copy-start.3 = (f32[64,128]{1,0:T(8,128)S(1)}, f32[64,128]{1,0:T(8,128)}, u32[]{:S(2)}) copy-start(f32[64,128]{1,0:T(8,128)} %param.11) | copy-start | bytes 98308
  3.6 48.9 %copy-start.4 = (f32[64,128]{1,0:T(8,128)S(1)}, f32[64,128]{1,0:T(8,128)}, u32[]{:S(2)}) copy-start(f32[64,128]{1,0:T(8,128)} %param.13) | copy-start | bytes 98308
  3.6 48.9 %copy-start.5 = (f32[64,128]{1,0:T(8,128)S(1)}, f32[64,128]{1,0:T(8,128)}, u32[]{:S(2)}) copy-start(f32[64,128]{1,0:T(8,128)} %param.12) | copy-start | bytes 98308
  34.7 5.1 %collective-permute-start = (f32[256,128]{1,0:T(8,128)S(1)}, f32[256,128]{1,0:T(8,128)S(1)}, u32[]{:S(2)}, u32[]{:S(2)}) collective-permute-start(f32[256,128]{1,0:T(8,128)S(1)} %get-tuple-element.10), channel_id=1, source_target_pairs={{0,2},{2,0},{4,6},{6,4},{8,10},{10,8},{12,14},{14,12},{1,3},{3,1},... | collective-permute-start | bytes 393224 | tf_op jit(solution)/shard_map/ppermute | solution.py:100
  39.8 8.6 %collective-permute-start.1 = (f32[64,128]{1,0:T(8,128)S(1)}, f32[64,128]{1,0:T(8,128)S(1)}, u32[]{:S(2)}, u32[]{:S(2)}) collective-permute-start(f32[64,128]{1,0:T(8,128)S(1)} %get-tuple-element.15), channel_id=1, source_target_pairs={{0,8},{2,10},{4,12},{6,14},{8,0},{10,2},{12,4},{14,6},{1,9},{3,11}... | collective-permute-start | bytes 98312 | tf_op jit(solution)/shard_map/ppermute | solution.py:100
  46.5 6.0 %collective-permute-start.3 = (f32[64,128]{1,0:T(8,128)S(1)}, f32[64,128]{1,0:T(8,128)S(1)}, u32[]{:S(2)}, u32[]{:S(2)}) collective-permute-start(f32[64,128]{1,0:T(8,128)S(1)} %get-tuple-element.16), channel_id=1, source_target_pairs={{0,12},{2,14},{4,8},{6,10},{8,4},{10,6},{12,0},{14,2},{1,13},{3,15... | collective-permute-start | bytes 98312 | tf_op jit(solution)/shard_map/ppermute | solution.py:100
  46.7 5.8 %collective-permute-start.2 = (f32[64,128]{1,0:T(8,128)S(1)}, f32[64,128]{1,0:T(8,128)S(1)}, u32[]{:S(2)}, u32[]{:S(2)}) collective-permute-start(f32[64,128]{1,0:T(8,128)S(1)} %get-tuple-element.17), channel_id=1, source_target_pairs={{0,4},{2,6},{4,0},{6,2},{8,12},{10,14},{12,8},{14,10},{1,5},{3,7},... | collective-permute-start | bytes 98312 | tf_op jit(solution)/shard_map/ppermute | solution.py:100

commit v2 on v1

--- a/solution.py
+++ b/solution.py
@@ -19,44 +19,77 @@
     return jnp.where(row == ids, 1.0, 0.0).astype(jnp.bfloat16)
 
 
-def pack_kernel(counts, picked, gradient, feedback, tiles, new_feedback):
-    owner = pl.program_id(0)
-    slots = picked.shape[-1]
-    rows, width = gradient.shape[2:]
-    compensated = gradient[0, 0].astype(jnp.float32) + feedback[0, 0]
+def pack_kernel(chunks, counts_in, picked_in, gradient, feedback, tiles, new_feedback, near, counts, picked, sems):
+    owners, slots = picked.shape[2:]
+    blocks, width = near.shape
+    rows = blocks // owners
+    step_rows = blocks // chunks
+
+    def copies(chunk):
+        here = pl.ds(pl.multiple_of(chunk * step_rows, step_rows), step_rows)
+        return (
+            pltpu.make_async_copy(gradient.at[0, 0, here, :], near.at[here, :], sems.at[0, chunk]),
+            pltpu.make_async_copy(feedback.at[0, 0, here, :], new_feedback.at[0, 0, here, :], sems.at[1, chunk]),
+        )
+
+    lists = (
+        pltpu.make_async_copy(counts_in, counts, sems.at[2, 0]),
+        pltpu.make_async_copy(picked_in, picked, sems.at[2, 1]),
+    )
+    for copy in lists:
+        copy.start()
+    for chunk in range(chunks):
+        for copy in copies(chunk):
+            copy.start()
+    for copy in lists:
+        copy.wait()
     slot = lax.broadcasted_iota(jnp.int32, (1, slots), 1)
-    ids = jnp.where(slot < counts[0, 0, owner], picked[0, 0, pl.ds(owner, 1), :], -1)
-    hot = one_hot(rows, ids)
-    named = jnp.dot(hot, jnp.ones((slots, width), jnp.bfloat16), preferred_element_type=jnp.float32)
-    new_feedback[0, 0] = jnp.where(named > 0.0, 0.0, compensated)
-    halves = lax.dot_general(hot, split(compensated), (((0,), (0,)), ((), ())), preferred_element_type=jnp.float32)
-    tiles[0, :slots, :] = halves[:, :width] + halves[:, width:]
-    sent = ids.astype(jnp.float32)
-    tiles[0, slots:, :] = jnp.broadcast_to(jnp.concatenate([sent, sent], axis=1), (tiles.shape[1] - slots, width))
+
+    def step(chunk, carry):
+        for copy in copies(chunk):
+            copy.wait()
+        for part in range(owners // chunks):
+            owner = chunk * (owners // chunks) + part
+            here = pl.ds(pl.multiple_of(owner * rows, rows), rows)
+            compensated = near[here, :].astype(jnp.float32) + new_feedback[0, 0, here, :]
+            ids = jnp.where(slot < counts[0, 0, owner], picked[0, 0, pl.ds(owner, 1), :], -1)
+            hot = one_hot(rows, ids)
+            named = jnp.dot(hot, jnp.ones((slots, width), jnp.bfloat16), preferred_element_type=jnp.float32)
+            new_feedback[0, 0, here, :] = jnp.where(named > 0.0, 0.0, compensated)
+            halves = lax.dot_general(
+                hot, split(compensated), (((0,), (0,)), ((), ())), preferred_element_type=jnp.float32
+            )
+            tiles[owner, :slots, :] = halves[:, :width] + halves[:, width:]
+            sent = ids.astype(jnp.float32)
+            sent = jnp.concatenate([sent, sent], axis=1)
+            tiles[owner, slots:, :] = jnp.broadcast_to(sent, (tiles.shape[1] - slots, width))
+        return carry
+
+    lax.fori_loop(0, chunks, step, 0)
 
 
 def pack(counts, picked, gradient, feedback):
     owners, slots = picked.shape[2:]
     blocks, width = gradient.shape[2:]
-    rows = blocks // owners
-    whole = pl.BlockSpec((1, 1, rows, width), lambda o: (0, 0, o, 0))
+    chunks = 4
+    arrays = [pltpu.with_memory_space_constraint(array, pltpu.HBM) for array in (counts, picked, gradient, feedback)]
     return pl.pallas_call(
-        pack_kernel,
-        grid=(owners,),
-        in_specs=[
-            pl.BlockSpec(memory_space=pltpu.SMEM),
-            pl.BlockSpec((1, 1, owners, slots), lambda o: (0, 0, 0, 0)),
-            whole,
-            whole,
+        functools.partial(pack_kernel, chunks),
+        in_specs=[pl.BlockSpec(memory_space=pltpu.HBM)] * 4,
+        out_specs=[pl.BlockSpec(memory_space=pltpu.VMEM)] * 2,
+        out_shape=[
+            pltpu.VMEM((owners, slots + 8, width), jnp.float32),
+            pltpu.VMEM(feedback.shape, jnp.float32),
         ],
-        out_specs=[pl.BlockSpec((1, slots + 8, width), lambda o: (o, 0, 0)), whole],
-        out_shape=[
-            jax.ShapeDtypeStruct((owners, slots + 8, width), jnp.float32),
-            jax.ShapeDtypeStruct(feedback.shape, jnp.float32),
+        scratch_shapes=[
+            pltpu.VMEM((blocks, width), jnp.bfloat16),
+            pltpu.SMEM(counts.shape, jnp.int32),
+            pltpu.VMEM(picked.shape, jnp.int32),
+            pltpu.SemaphoreType.DMA((3, chunks)),
         ],
-        compiler_params=pltpu.CompilerParams(vmem_limit_bytes=48 * 2**20),
+        compiler_params=pltpu.CompilerParams(vmem_limit_bytes=32 * 2**20),
         name="pack",
-    )(counts, picked, gradient, feedback)
+    )(*arrays)
 
 
 def gather_sum_kernel(slots, rows, got, kept, sent, hot, parts):

time: 53.6 us -> 42.5 us (0.79)
  Pallas kernels: 12 us -> 4.12 us
  waiting for transfers between devices: 9.06 us -> 7.04 us
  local copies, waits for them, and re-layouts: 2.95 us -> 2.03 us
    pallas_call x1, Pallas kernels: 11.4 us -> 3.54 us  [pack(): pl.pallas_call(functools.partial(pack_kernel, chunks), in_specs=[pl.Block...]
    ppermute x4, waiting for transfers between devices: 9.06 us -> 7.04 us  [swapped(): lax.ppermute(value, 'replica', [(source, source ^ mask) for source in ran...]
    unnamed x12 -> x7, local copies, waits for them, and re-layouts: 2.95 us -> 2.02 us
  transfers between devices with their start and end apart: 4 -> 4, of which waited for: 3 -> 2; matrix products, arithmetic and copies ran while one was open for 0% -> 5% of each run, Pallas kernels for 0% -> 0%
where the time goes in v2:
time: 42.5 us; the launch traced here: 42.3 us
  blocking collectives  19.1 us (45%)
  starting transfers between devices  8.75 us (21%)
  waiting for transfers between devices  7.04 us (17%)
  Pallas kernels  4.12 us (10%)
  local copies, waits for them, and re-layouts  2.03 us (5%)
  other arithmetic  0.68 us (2%)
  between operations  0.67 us (2%)
    all_to_all x1, blocking collectives, body(): lax.all_to_all(tiles, 'region', split_axis=0, concat_axis=0, tiled=True)  19.1 us
    ppermute x4, starting transfers between devices, swapped(): lax.ppermute(value, 'replica', [(source, source ^ mask) for source in ran...  8.75 us
    ppermute x4, waiting for transfers between devices, swapped(): lax.ppermute(value, 'replica', [(source, source ^ mask) for source in ran...  7.04 us
    pallas_call x1, Pallas kernels, pack(): pl.pallas_call(functools.partial(pack_kernel, chunks), in_specs=[pl.Block...  3.54 us
    unnamed x7, local copies, waits for them, and re-layouts  2.02 us
  transfers between devices with their start and end apart: 4, of which 2 were waited for; matrix products, arithmetic and copies ran while one was open for 5% of the time, Pallas kernels for 0%

profile of v2, /device:TPU:32, one launch (start us, length us, event | category | flops | bytes accessed | tf_op | source)
XLA Modules:
  0.0 42.3 jit_solution(9693353887256141127)
XLA Ops:
  0.6 3.5 %pack.1 = (f32[16,72,128]{2,1,0:T(8,128)S(1)}, f32[1,1,8192,128]{3,2,1,0:T(8,128)S(1)}) custom-call(s32[1,1,16]{2,1,0:T(1,128)} %counts_in.1, s32[1,1,16,64]{3,2,1,0:T(8,128)} %picked_in.1, bf16[1,1,8192,128]{3,2,1,0:T(8,128)(2,1)} %gradient.1, f32[1,1,8192,128]{3,2,1,0:T(8,128)} %feedback.1), custom_call_target="tpu_custom_call" | custom-call | tf_op jit(solution)/shard_map/pack/pallas_call | solution.py:76
  4.2 19.1 %all_to_all.5.got = f32[16,72,128]{2,1,0:T(8,128)S(1)} all-to-all(f32[16,72,128]{2,1,0:T(8,128)S(1)} %get-tuple-element.8), channel_id=1, replica_groups=mesh['region'=16,'replica'=8,'tensor'=2] {'region'}, dimensions={0} | all-to-all | bytes 1179648 | tf_op jit(solution)/shard_map/all_to_all | solution.py:140
  23.2 0.6 %gather_sum.1 = (f32[256,128]{1,0:T(8,128)S(1)}, f32[256,128]{1,0:T(8,128)S(1)}) custom-call(f32[16,72,128]{2,1,0:T(8,128)S(1)} %all_to_all.5.got), custom_call_target="tpu_custom_call" | custom-call | tf_op jit(solution)/shard_map/gather_sum/pallas_call | solution.py:118
  23.8 0.2 collective-permute-start
  24.0 4.9 %collective-permute-done = f32[256,128]{1,0:T(8,128)S(1)} collective-permute-done((f32[256,128]{1,0:T(8,128)S(1)}, f32[256,128]{1,0:T(8,128)S(1)}, u32[]{:S(2)}, u32[]{:S(2)}) %collective-permute-start) | collective-permute-done | bytes 131104 | tf_op jit(solution)/shard_map/ppermute | solution.py:133
  28.9 6.7 %collective-permute-start.1 = (f32[64,128]{1,0:T(8,128)S(1)}, f32[64,128]{1,0:T(8,128)S(1)}, u32[]{:S(2)}, u32[]{:S(2)}) collective-permute-start(f32[64,128]{1,0:T(8,128)S(1)} %get-tuple-element.15), channel_id=1, source_target_pairs={{0,8},{2,10},{4,12},{6,14},{8,0},{10,2},{12,4},{14,6},{1,9},{3,11}... | collective-permute-start | bytes 98312 | tf_op jit(solution)/shard_map/ppermute | solution.py:133
  35.6 0.2 collective-permute-start.3
  35.8 1.6 %collective-permute-start.2 = (f32[64,128]{1,0:T(8,128)S(1)}, f32[64,128]{1,0:T(8,128)S(1)}, u32[]{:S(2)}, u32[]{:S(2)}) collective-permute-start(f32[64,128]{1,0:T(8,128)S(1)} %get-tuple-element.17), channel_id=1, source_target_pairs={{0,4},{2,6},{4,0},{6,2},{8,12},{10,14},{12,8},{14,10},{1,5},{3,7},... | collective-permute-start | bytes 98312 | tf_op jit(solution)/shard_map/ppermute | solution.py:133
  37.5 0.0 copy-start
  37.5 0.0 copy-start.1
  37.5 0.0 copy-start.2
  37.5 2.0 %copy.11 = f32[1,1,8192,128]{3,2,1,0:T(8,128)} copy(f32[1,1,8192,128]{3,2,1,0:T(8,128)S(1)} %get-tuple-element.21) | data formatting | bytes 8388608
  39.5 0.0 collective-permute-done.1
  39.5 2.2 %collective-permute-done.3 = f32[64,128]{1,0:T(8,128)S(1)} collective-permute-done((f32[64,128]{1,0:T(8,128)S(1)}, f32[64,128]{1,0:T(8,128)S(1)}, u32[]{:S(2)}, u32[]{:S(2)}) %collective-permute-start.3) | collective-permute-done | bytes 32800 | tf_op jit(solution)/shard_map/ppermute | solution.py:133
  41.7 0.0 collective-permute-done.2
  41.7 0.0 copy-done
  41.7 0.0 copy-done.1
  41.7 0.0 copy-done.2
  41.7 0.7 %multiply_subtract_fusion = (f32[64,128]{1,0:T(8,128)}, f32[64,128]{1,0:T(8,128)}, f32[64,128]{1,0:T(8,128)}) fusion(f32[64,128]{1,0:T(8,128)S(1)} %copy-done, f32[64,128]{1,0:T(8,128)S(1)} %copy-done.1, f32[64,128]{1,0:T(8,128)S(1)} %copy-done.2, f32[64,128]{1,0:T(8,128)S(1)} %collective-permute-done.3, f32[64,128]{1,0:T(8,128)S(1)} %collective-permute-done.2, ...), kind=kLoop, calls=%fused_computation.5 | loop fusion | flops 131072 | bytes 327680 | tf_op jit(solution)/shard_map/sub | solution.py:147
  (2 shorter events, 0.0 us)
Async XLA Ops:
  23.8 5.1 %collective-permute-start = (f32[256,128]{1,0:T(8,128)S(1)}, f32[256,128]{1,0:T(8,128)S(1)}, u32[]{:S(2)}, u32[]{:S(2)}) collective-permute-start(f32[256,128]{1,0:T(8,128)S(1)} %get-tuple-element.10), channel_id=1, source_target_pairs={{0,2},{2,0},{4,6},{6,4},{8,10},{10,8},{12,14},{14,12},{1,3},{3,1},... | collective-permute-start | bytes 393224 | tf_op jit(solution)/shard_map/ppermute | solution.py:133
  28.9 10.6 %collective-permute-start.1 = (f32[64,128]{1,0:T(8,128)S(1)}, f32[64,128]{1,0:T(8,128)S(1)}, u32[]{:S(2)}, u32[]{:S(2)}) collective-permute-start(f32[64,128]{1,0:T(8,128)S(1)} %get-tuple-element.15), channel_id=1, source_target_pairs={{0,8},{2,10},{4,12},{6,14},{8,0},{10,2},{12,4},{14,6},{1,9},{3,11}... | collective-permute-start | bytes 98312 | tf_op jit(solution)/shard_map/ppermute | solution.py:133
  35.6 6.0 %collective-permute-start.3 = (f32[64,128]{1,0:T(8,128)S(1)}, f32[64,128]{1,0:T(8,128)S(1)}, u32[]{:S(2)}, u32[]{:S(2)}) collective-permute-start(f32[64,128]{1,0:T(8,128)S(1)} %get-tuple-element.16), channel_id=1, source_target_pairs={{0,12},{2,14},{4,8},{6,10},{8,4},{10,6},{12,0},{14,2},{1,13},{3,15... | collective-permute-start | bytes 98312 | tf_op jit(solution)/shard_map/ppermute | solution.py:133
  35.8 5.8 %collective-permute-start.2 = (f32[64,128]{1,0:T(8,128)S(1)}, f32[64,128]{1,0:T(8,128)S(1)}, u32[]{:S(2)}, u32[]{:S(2)}) collective-permute-start(f32[64,128]{1,0:T(8,128)S(1)} %get-tuple-element.17), channel_id=1, source_target_pairs={{0,4},{2,6},{4,0},{6,2},{8,12},{10,14},{12,8},{14,10},{1,5},{3,7},... | collective-permute-start | bytes 98312 | tf_op jit(solution)/shard_map/ppermute | solution.py:133
  37.5 4.2 %copy-start = (f32[64,128]{1,0:T(8,128)S(1)}, f32[64,128]{1,0:T(8,128)}, u32[]{:S(2)}) copy-start(f32[64,128]{1,0:T(8,128)} %param.11) | copy-start | bytes 98308
  37.5 4.2 %copy-start.1 = (f32[64,128]{1,0:T(8,128)S(1)}, f32[64,128]{1,0:T(8,128)}, u32[]{:S(2)}) copy-start(f32[64,128]{1,0:T(8,128)} %param.13) | copy-start | bytes 98308
  37.5 4.2 %copy-start.2 = (f32[64,128]{1,0:T(8,128)S(1)}, f32[64,128]{1,0:T(8,128)}, u32[]{:S(2)}) copy-start(f32[64,128]{1,0:T(8,128)} %param.12) | copy-start | bytes 98308

commit v3 on v2

--- a/solution.py
+++ b/solution.py
@@ -92,39 +92,44 @@
     )(*arrays)
 
 
-def gather_sum_kernel(slots, rows, got, kept, sent, hot, parts):
+def gather_sum_kernel(slots, rows, got, kept_first, kept, sent_first, sent, hot, parts):
     me = lax.axis_index("replica")
     sources, _, width = got.shape
+    block = kept_first.shape[0]
     lane = lax.broadcasted_iota(jnp.int32, (1, 2 * slots), 1)
     for pair in range(sources // 2):
         first, second = 2 * pair, 2 * pair + 1
         ids = jnp.where(lane < slots, got[first, slots : slots + 1, :], got[second, slots : slots + 1, :])
         ids = ids.astype(jnp.int32)
         far = (ids >> 6) ^ me
-        place = jnp.where(ids < 0, -1, ((far & 1) << 8) | ((far >> 1) << 6) | (ids & 63))
+        two, one = far >> 2, (far >> 1) & 1
+        away = (far & 1) ^ two ^ (two & one)
+        place = jnp.where(ids < 0, -1, (away << 8) | (one << 7) | ((1 - two) << 6) | (ids & 63))
         hot[:, pair * 2 * slots : (pair + 1) * 2 * slots] = one_hot(rows, place)
         for source in (first, second):
             parts[source * slots : (source + 1) * slots, :] = split(got[source, :slots, :])
     halves = jnp.dot(hot[...], parts[...], preferred_element_type=jnp.float32)
     total = halves[:, :width] + halves[:, width:]
-    kept[...] = total[: rows // 2]
-    sent[...] = total[rows // 2 :]
+    kept_first[...] = total[:block]
+    kept[...] = total[block : rows // 2]
+    sent_first[...] = total[rows // 2 : rows // 2 + block]
+    sent[...] = total[rows // 2 + block :]
 
 
 def gather_sum(got, rows):
     sources, _, width = got.shape
     slots = width // 2
-    half = jax.ShapeDtypeStruct((rows // 2, width), jnp.float32)
+    shapes = [jax.ShapeDtypeStruct((rows // 4, width), jnp.float32)] * 4
     return pl.pallas_call(
         functools.partial(gather_sum_kernel, slots, rows),
         in_specs=[pl.BlockSpec(memory_space=pltpu.VMEM)],
-        out_specs=[pl.BlockSpec(memory_space=pltpu.VMEM)] * 2,
-        out_shape=[half, half],
+        out_specs=[pl.BlockSpec(memory_space=pltpu.VMEM)] * 4,
+        out_shape=shapes,
         scratch_shapes=[
             pltpu.VMEM((rows, sources * slots), jnp.bfloat16),
             pltpu.VMEM((sources * slots, 2 * width), jnp.bfloat16),
         ],
-        compiler_params=pltpu.CompilerParams(vmem_limit_bytes=48 * 2**20),
+        compiler_params=pltpu.CompilerParams(vmem_limit_bytes=16 * 2**20),
         name="gather_sum",
     )(got)
 
@@ -138,10 +143,10 @@
     reg_rows = own_rows * lax.axis_size("replica")
     tiles, new_feedback = pack(counts, picked, gradient, feedback)
     got = lax.all_to_all(tiles, "region", split_axis=0, concat_axis=0, tiled=True)
-    kept, sent = gather_sum(got, reg_rows)
-    part = (kept + swapped(sent, 1)).reshape(4, own_rows, kept.shape[1])
-    far = [swapped(part[pair], 2 * pair) for pair in (2, 1, 3)]
-    total = part[0] + far[0] + far[1] + far[2]
+    kept_first, kept, sent_first, sent = gather_sum(got, reg_rows)
+    five, own = jnp.split(kept_first + swapped(sent_first, 1), 2)
+    six, two = jnp.split(kept + swapped(sent, 1), 2)
+    total = own + swapped(five, 5) + swapped(six, 6) + swapped(two, 2)
     new_moment = 0.9 * moment + 0.1 * total
     new_second = 0.95 * second + 0.05 * total * total
     new_weights = weights - 0.02 * (new_moment / (jnp.sqrt(new_second) + 1e-08) + 0.1 * weights)

time: 42.5 us -> 41.1 us (0.967)
  waiting for transfers between devices: 7.04 us -> 4.34 us
  starting transfers between devices: 8.75 us -> 10 us
    ppermute x4 -> x5, waiting for transfers between devices: 7.04 us -> 4.34 us  [swapped(): lax.ppermute(value, 'replica', [(source, source ^ mask) for source in ran...]
    ppermute x4 -> x5, starting transfers between devices: 8.75 us -> 10 us  [swapped(): lax.ppermute(value, 'replica', [(source, source ^ mask) for source in ran...]
  transfers between devices with their start and end apart: 4 -> 5, of which waited for: 2 -> 2; matrix products, arithmetic and copies ran while one was open for 5% -> 5% of each run, Pallas kernels for 0% -> 0%
where the time goes in v3:
time: 41.1 us; the launch traced here: 41 us
  blocking collectives  19.1 us (46%)
  starting transfers between devices  10 us (24%)
  waiting for transfers between devices  4.34 us (11%)
  Pallas kernels  4.13 us (10%)
  local copies, waits for them, and re-layouts  2.03 us (5%)
  between operations  0.69 us (2%)
  other arithmetic  0.67 us (2%)
    all_to_all x1, blocking collectives, body(): lax.all_to_all(tiles, 'region', split_axis=0, concat_axis=0, tiled=True)  19.1 us
    ppermute x5, starting transfers between devices, swapped(): lax.ppermute(value, 'replica', [(source, source ^ mask) for source in ran...  10 us
    ppermute x5, waiting for transfers between devices, swapped(): lax.ppermute(value, 'replica', [(source, source ^ mask) for source in ran...  4.34 us
    pallas_call x1, Pallas kernels, pack(): pl.pallas_call(functools.partial(pack_kernel, chunks), in_specs=[pl.Block...  3.54 us
    unnamed x7, local copies, waits for them, and re-layouts  2.02 us
  transfers between devices with their start and end apart: 5, of which 2 were waited for; matrix products, arithmetic and copies ran while one was open for 5% of the time, Pallas kernels for 0%

profile of v3, /device:TPU:32, one launch (start us, length us, event | category | flops | bytes accessed | tf_op | source)
XLA Modules:
  0.0 41.0 jit_solution(13813667634636950725)
XLA Ops:
  0.6 3.5 %pack.1 = (f32[16,72,128]{2,1,0:T(8,128)S(1)}, f32[1,1,8192,128]{3,2,1,0:T(8,128)S(1)}) custom-call(s32[1,1,16]{2,1,0:T(1,128)} %counts_in.1, s32[1,1,16,64]{3,2,1,0:T(8,128)} %picked_in.1, bf16[1,1,8192,128]{3,2,1,0:T(8,128)(2,1)} %gradient.1, f32[1,1,8192,128]{3,2,1,0:T(8,128)} %feedback.1), custom_call_target="tpu_custom_call" | custom-call | tf_op jit(solution)/shard_map/pack/pallas_call | solution.py:76
  4.2 19.1 %all_to_all.5.got = f32[16,72,128]{2,1,0:T(8,128)S(1)} all-to-all(f32[16,72,128]{2,1,0:T(8,128)S(1)} %get-tuple-element.10), channel_id=1, replica_groups=mesh['region'=16,'replica'=8,'tensor'=2] {'region'}, dimensions={0} | all-to-all | bytes 1179648 | tf_op jit(solution)/shard_map/all_to_all | solution.py:145
  23.2 0.6 %gather_sum.1 = (f32[128,128]{1,0:T(8,128)S(1)}, f32[128,128]{1,0:T(8,128)S(1)}, f32[128,128]{1,0:T(8,128)S(1)}, f32[128,128]{1,0:T(8,128)S(1)}) custom-call(f32[16,72,128]{2,1,0:T(8,128)S(1)} %all_to_all.5.got), custom_call_target="tpu_custom_call" | custom-call | tf_op jit(solution)/shard_map/gather_sum/pallas_call | solution.py:123
  23.8 0.2 collective-permute-start
  24.0 1.9 %collective-permute-start.2 = (f32[128,128]{1,0:T(8,128)S(1)}, f32[128,128]{1,0:T(8,128)S(1)}, u32[]{:S(2)}, u32[]{:S(2)}) collective-permute-start(f32[128,128]{1,0:T(8,128)S(1)} %get-tuple-element.14), channel_id=1, source_target_pairs={{0,2},{2,0},{4,6},{6,4},{8,10},{10,8},{12,14},{14,12},{1,3},{3,1},... | collective-permute-start | bytes 196616 | tf_op jit(solution)/shard_map/ppermute | solution.py:138
  25.9 2.2 %collective-permute-done = f32[128,128]{1,0:T(8,128)S(1)} collective-permute-done((f32[128,128]{1,0:T(8,128)S(1)}, f32[128,128]{1,0:T(8,128)S(1)}, u32[]{:S(2)}, u32[]{:S(2)}) %collective-permute-start) | collective-permute-done | bytes 65568 | tf_op jit(solution)/shard_map/ppermute | solution.py:138
  28.2 5.9 %collective-permute-start.1 = (f32[64,128]{1,0:T(8,128)S(1)}, f32[64,128]{1,0:T(8,128)S(1)}, u32[]{:S(2)}, u32[]{:S(2)}) collective-permute-start(f32[64,128]{1,0:T(8,128)S(1)} %split.17), channel_id=1, source_target_pairs={{0,10},{2,8},{4,14},{6,12},{8,2},{10,0},{12,6},{14,4},{1,11},{3,9}... | collective-permute-start | bytes 98312 | tf_op jit(solution)/shard_map/ppermute | solution.py:138
  34.1 0.0 collective-permute-done.2
  34.2 0.6 %collective-permute-start.3 = (f32[64,128]{1,0:T(8,128)S(1)}, f32[64,128]{1,0:T(8,128)S(1)}, u32[]{:S(2)}, u32[]{:S(2)}) collective-permute-start(f32[64,128]{1,0:T(8,128)S(1)} %get-tuple-element.19), channel_id=1, source_target_pairs={{0,12},{2,14},{4,8},{6,10},{8,4},{10,6},{12,0},{14,2},{1,13},{3,15... | collective-permute-start | bytes 98312 | tf_op jit(solution)/shard_map/ppermute | solution.py:138
  34.7 1.4 %collective-permute-start.4 = (f32[64,128]{1,0:T(8,128)S(1)}, f32[64,128]{1,0:T(8,128)S(1)}, u32[]{:S(2)}, u32[]{:S(2)}) collective-permute-start(f32[64,128]{1,0:T(8,128)S(1)} %get-tuple-element.20), channel_id=1, source_target_pairs={{0,4},{2,6},{4,0},{6,2},{8,12},{10,14},{12,8},{14,10},{1,5},{3,7},... | collective-permute-start | bytes 98312 | tf_op jit(solution)/shard_map/ppermute | solution.py:138
  36.2 0.0 copy-start
  36.2 0.0 copy-start.1
  36.2 0.0 copy-start.2
  36.2 2.0 %copy.11 = f32[1,1,8192,128]{3,2,1,0:T(8,128)} copy(f32[1,1,8192,128]{3,2,1,0:T(8,128)S(1)} %get-tuple-element.24) | data formatting | bytes 8388608
  38.2 0.0 collective-permute-done.1
  38.2 2.1 %collective-permute-done.3 = f32[64,128]{1,0:T(8,128)S(1)} collective-permute-done((f32[64,128]{1,0:T(8,128)S(1)}, f32[64,128]{1,0:T(8,128)S(1)}, u32[]{:S(2)}, u32[]{:S(2)}) %collective-permute-start.3) | collective-permute-done | bytes 32800 | tf_op jit(solution)/shard_map/ppermute | solution.py:138
  40.3 0.0 collective-permute-done.4
  40.3 0.0 copy-done
  40.3 0.0 copy-done.1
  40.3 0.0 copy-done.2
  40.3 0.7 %multiply_subtract_fusion = (f32[64,128]{1,0:T(8,128)}, f32[64,128]{1,0:T(8,128)}, f32[64,128]{1,0:T(8,128)}) fusion(f32[64,128]{1,0:T(8,128)S(1)} %copy-done, f32[64,128]{1,0:T(8,128)S(1)} %copy-done.1, f32[64,128]{1,0:T(8,128)S(1)} %copy-done.2, f32[64,128]{1,0:T(8,128)S(1)} %collective-permute-done.4, f32[64,128]{1,0:T(8,128)S(1)} %collective-permute-done.3, ...), kind=kLoop, calls=%fused_computation.5 | loop fusion | flops 131072 | bytes 327680 | tf_op jit(solution)/shard_map/sub | solution.py:152
  (4 shorter events, 0.0 us)
Async XLA Ops:
  23.8 4.4 %collective-permute-start = (f32[128,128]{1,0:T(8,128)S(1)}, f32[128,128]{1,0:T(8,128)S(1)}, u32[]{:S(2)}, u32[]{:S(2)}) collective-permute-start(f32[128,128]{1,0:T(8,128)S(1)} %get-tuple-element.12), channel_id=1, source_target_pairs={{0,2},{2,0},{4,6},{6,4},{8,10},{10,8},{12,14},{14,12},{1,3},{3,1},... | collective-permute-start | bytes 196616 | tf_op jit(solution)/shard_map/ppermute | solution.py:138
  24.0 10.1 %collective-permute-start.2 = (f32[128,128]{1,0:T(8,128)S(1)}, f32[128,128]{1,0:T(8,128)S(1)}, u32[]{:S(2)}, u32[]{:S(2)}) collective-permute-start(f32[128,128]{1,0:T(8,128)S(1)} %get-tuple-element.14), channel_id=1, source_target_pairs={{0,2},{2,0},{4,6},{6,4},{8,10},{10,8},{12,14},{14,12},{1,3},{3,1},... | collective-permute-start | bytes 196616 | tf_op jit(solution)/shard_map/ppermute | solution.py:138
  28.2 10.0 %collective-permute-start.1 = (f32[64,128]{1,0:T(8,128)S(1)}, f32[64,128]{1,0:T(8,128)S(1)}, u32[]{:S(2)}, u32[]{:S(2)}) collective-permute-start(f32[64,128]{1,0:T(8,128)S(1)} %split.17), channel_id=1, source_target_pairs={{0,10},{2,8},{4,14},{6,12},{8,2},{10,0},{12,6},{14,4},{1,11},{3,9}... | collective-permute-start | bytes 98312 | tf_op jit(solution)/shard_map/ppermute | solution.py:138
  34.2 6.1 %collective-permute-start.3 = (f32[64,128]{1,0:T(8,128)S(1)}, f32[64,128]{1,0:T(8,128)S(1)}, u32[]{:S(2)}, u32[]{:S(2)}) collective-permute-start(f32[64,128]{1,0:T(8,128)S(1)} %get-tuple-element.19), channel_id=1, source_target_pairs={{0,12},{2,14},{4,8},{6,10},{8,4},{10,6},{12,0},{14,2},{1,13},{3,15... | collective-permute-start | bytes 98312 | tf_op jit(solution)/shard_map/ppermute | solution.py:138
  34.7 5.5 %collective-permute-start.4 = (f32[64,128]{1,0:T(8,128)S(1)}, f32[64,128]{1,0:T(8,128)S(1)}, u32[]{:S(2)}, u32[]{:S(2)}) collective-permute-start(f32[64,128]{1,0:T(8,128)S(1)} %get-tuple-element.20), channel_id=1, source_target_pairs={{0,4},{2,6},{4,0},{6,2},{8,12},{10,14},{12,8},{14,10},{1,5},{3,7},... | collective-permute-start | bytes 98312 | tf_op jit(solution)/shard_map/ppermute | solution.py:138
  36.2 4.1 %copy-start = (f32[64,128]{1,0:T(8,128)S(1)}, f32[64,128]{1,0:T(8,128)}, u32[]{:S(2)}) copy-start(f32[64,128]{1,0:T(8,128)} %param.11) | copy-start | bytes 98308
  36.2 4.1 %copy-start.1 = (f32[64,128]{1,0:T(8,128)S(1)}, f32[64,128]{1,0:T(8,128)}, u32[]{:S(2)}) copy-start(f32[64,128]{1,0:T(8,128)} %param.13) | copy-start | bytes 98308
  36.2 4.1 %copy-start.2 = (f32[64,128]{1,0:T(8,128)S(1)}, f32[64,128]{1,0:T(8,128)}, u32[]{:S(2)}) copy-start(f32[64,128]{1,0:T(8,128)} %param.12) | copy-start | bytes 98308

commit v4 on v2

--- a/solution.py
+++ b/solution.py
@@ -92,39 +92,45 @@
     )(*arrays)
 
 
-def gather_sum_kernel(slots, rows, got, kept, sent, hot, parts):
+def gather_sum_kernel(slots, blocks, got, hot, parts, *sums):
     me = lax.axis_index("replica")
     sources, _, width = got.shape
+    rows = hot.shape[0]
+    own_rows = rows // 8
     lane = lax.broadcasted_iota(jnp.int32, (1, 2 * slots), 1)
     for pair in range(sources // 2):
         first, second = 2 * pair, 2 * pair + 1
         ids = jnp.where(lane < slots, got[first, slots : slots + 1, :], got[second, slots : slots + 1, :])
         ids = ids.astype(jnp.int32)
-        far = (ids >> 6) ^ me
-        place = jnp.where(ids < 0, -1, ((far & 1) << 8) | ((far >> 1) << 6) | (ids & 63))
+        place = jnp.where(ids < 0, -1, ids ^ (me * own_rows))
         hot[:, pair * 2 * slots : (pair + 1) * 2 * slots] = one_hot(rows, place)
         for source in (first, second):
             parts[source * slots : (source + 1) * slots, :] = split(got[source, :slots, :])
     halves = jnp.dot(hot[...], parts[...], preferred_element_type=jnp.float32)
     total = halves[:, :width] + halves[:, width:]
-    kept[...] = total[: rows // 2]
-    sent[...] = total[rows // 2 :]
+    for group, ref in zip(blocks, sums):
+        for position, block in enumerate(group):
+            here = slice(position * own_rows, (position + 1) * own_rows)
+            ref[here, :] = total[block * own_rows : (block + 1) * own_rows]
 
 
-def gather_sum(got, rows):
+def gather_sum(got, rows, blocks):
     sources, _, width = got.shape
     slots = width // 2
-    half = jax.ShapeDtypeStruct((rows // 2, width), jnp.float32)
+
+    def kernel(got, *refs):
+        gather_sum_kernel(slots, blocks, got, *refs[-2:], *refs[:-2])
+
     return pl.pallas_call(
-        functools.partial(gather_sum_kernel, slots, rows),
+        kernel,
         in_specs=[pl.BlockSpec(memory_space=pltpu.VMEM)],
-        out_specs=[pl.BlockSpec(memory_space=pltpu.VMEM)] * 2,
-        out_shape=[half, half],
+        out_specs=[pl.BlockSpec(memory_space=pltpu.VMEM)] * len(blocks),
+        out_shape=[pltpu.VMEM((len(group) * rows // 8, width), jnp.float32) for group in blocks],
         scratch_shapes=[
             pltpu.VMEM((rows, sources * slots), jnp.bfloat16),
             pltpu.VMEM((sources * slots, 2 * width), jnp.bfloat16),
         ],
-        compiler_params=pltpu.CompilerParams(vmem_limit_bytes=48 * 2**20),
+        compiler_params=pltpu.CompilerParams(vmem_limit_bytes=16 * 2**20),
         name="gather_sum",
     )(got)
 
@@ -138,10 +144,11 @@
     reg_rows = own_rows * lax.axis_size("replica")
     tiles, new_feedback = pack(counts, picked, gradient, feedback)
     got = lax.all_to_all(tiles, "region", split_axis=0, concat_axis=0, tiled=True)
-    kept, sent = gather_sum(got, reg_rows)
-    part = (kept + swapped(sent, 1)).reshape(4, own_rows, kept.shape[1])
-    far = [swapped(part[pair], 2 * pair) for pair in (2, 1, 3)]
-    total = part[0] + far[0] + far[1] + far[2]
+    five, near, four, six, two, three, own = gather_sum(got, reg_rows, ((5,), (7, 1), (4,), (6,), (2,), (3,), (0,)))
+    five = swapped(five, 3)
+    near = swapped(near, 1)
+    six = six + five + near[:own_rows] + swapped(four, 2)
+    total = own + near[own_rows:] + swapped(six, 6) + swapped(two, 2) + swapped(three, 3)
     new_moment = 0.9 * moment + 0.1 * total
     new_second = 0.95 * second + 0.05 * total * total
     new_weights = weights - 0.02 * (new_moment / (jnp.sqrt(new_second) + 1e-08) + 0.1 * weights)

time: 42.5 us -> 40.3 us (0.948)
  waiting for transfers between devices: 7.04 us -> 2.17 us
  starting transfers between devices: 8.75 us -> 11.5 us
    ppermute x4 -> x6, waiting for transfers between devices: 7.04 us -> 2.17 us  [swapped(): lax.ppermute(value, 'replica', [(source, source ^ mask) for source in ran...]
    ppermute x4 -> x6, starting transfers between devices: 8.75 us -> 11.5 us  [swapped(): lax.ppermute(value, 'replica', [(source, source ^ mask) for source in ran...]
  transfers between devices with their start and end apart: 4 -> 6, of which waited for: 2 -> 2; matrix products, arithmetic and copies ran while one was open for 5% -> 5% of each run, Pallas kernels for 0% -> 0%
where the time goes in v4:
time: 40.3 us; the launch traced here: 40.2 us
  blocking collectives  19.1 us (47%)
  starting transfers between devices  11.5 us (29%)
  Pallas kernels  4.1 us (10%)
  waiting for transfers between devices  2.17 us (5%)
  local copies, waits for them, and re-layouts  2.02 us (5%)
  between operations  0.68 us (2%)
  other arithmetic  0.67 us (2%)
    all_to_all x1, blocking collectives, body(): lax.all_to_all(tiles, 'region', split_axis=0, concat_axis=0, tiled=True)  19.1 us
    ppermute x6, starting transfers between devices, swapped(): lax.ppermute(value, 'replica', [(source, source ^ mask) for source in ran...  11.5 us
    pallas_call x1, Pallas kernels, pack(): pl.pallas_call(functools.partial(pack_kernel, chunks), in_specs=[pl.Block...  3.54 us
    ppermute x6, waiting for transfers between devices, swapped(): lax.ppermute(value, 'replica', [(source, source ^ mask) for source in ran...  2.17 us
    unnamed x7, local copies, waits for them, and re-layouts  2.02 us
  transfers between devices with their start and end apart: 6, of which 2 were waited for; matrix products, arithmetic and copies ran while one was open for 5% of the time, Pallas kernels for 0%

profile of v4, /device:TPU:32, one launch (start us, length us, event | category | flops | bytes accessed | tf_op | source)
XLA Modules:
  0.0 40.2 jit_solution(3943638499823698816)
XLA Ops:
  0.6 3.5 %pack.1 = (f32[16,72,128]{2,1,0:T(8,128)S(1)}, f32[1,1,8192,128]{3,2,1,0:T(8,128)S(1)}) custom-call(s32[1,1,16]{2,1,0:T(1,128)} %counts_in.1, s32[1,1,16,64]{3,2,1,0:T(8,128)} %picked_in.1, bf16[1,1,8192,128]{3,2,1,0:T(8,128)(2,1)} %gradient.1, f32[1,1,8192,128]{3,2,1,0:T(8,128)} %feedback.1), custom_call_target="tpu_custom_call" | custom-call | tf_op jit(solution)/shard_map/pack/pallas_call | solution.py:76
  4.2 19.1 %all_to_all.5.got = f32[16,72,128]{2,1,0:T(8,128)S(1)} all-to-all(f32[16,72,128]{2,1,0:T(8,128)S(1)} %get-tuple-element.13), channel_id=1, replica_groups=mesh['region'=16,'replica'=8,'tensor'=2] {'region'}, dimensions={0} | all-to-all | bytes 1179648 | tf_op jit(solution)/shard_map/all_to_all | solution.py:146
  23.2 0.6 %gather_sum.1 = (f32[64,128]{1,0:T(8,128)S(1)}, f32[128,128]{1,0:T(8,128)S(1)}, f32[64,128]{1,0:T(8,128)S(1)}, f32[64,128]{1,0:T(8,128)S(1)}, f32[64,128]{1,0:T(...) custom-call(f32[16,72,128]{2,1,0:T(8,128)S(1)} %all_to_all.5.got), custom_call_target="tpu_custom_call" | custom-call | tf_op jit(solution)/shard_map/gather_sum/pallas_call | solution.py:124
  23.8 0.2 collective-permute-start
  24.0 3.7 %collective-permute-start.1 = (f32[64,128]{1,0:T(8,128)S(1)}, f32[64,128]{1,0:T(8,128)S(1)}, u32[]{:S(2)}, u32[]{:S(2)}) collective-permute-start(f32[64,128]{1,0:T(8,128)S(1)} %get-tuple-element.17), channel_id=1, source_target_pairs={{0,6},{2,4},{4,2},{6,0},{8,14},{10,12},{12,10},{14,8},{1,7},{3,5},... | collective-permute-start | bytes 98312 | tf_op jit(solution)/shard_map/ppermute | solution.py:139
  27.7 0.5 %collective-permute-start.2 = (f32[64,128]{1,0:T(8,128)S(1)}, f32[64,128]{1,0:T(8,128)S(1)}, u32[]{:S(2)}, u32[]{:S(2)}) collective-permute-start(f32[64,128]{1,0:T(8,128)S(1)} %get-tuple-element.18), channel_id=1, source_target_pairs={{0,4},{2,6},{4,0},{6,2},{8,12},{10,14},{12,8},{14,10},{1,5},{3,7},... | collective-permute-start | bytes 98312 | tf_op jit(solution)/shard_map/ppermute | solution.py:139
  28.3 2.4 %collective-permute-start.4 = (f32[64,128]{1,0:T(8,128)S(1)}, f32[64,128]{1,0:T(8,128)S(1)}, u32[]{:S(2)}, u32[]{:S(2)}) collective-permute-start(f32[64,128]{1,0:T(8,128)S(1)} %get-tuple-element.19), channel_id=1, source_target_pairs={{0,4},{2,6},{4,0},{6,2},{8,12},{10,14},{12,8},{14,10},{1,5},{3,7},... | collective-permute-start | bytes 98312 | tf_op jit(solution)/shard_map/ppermute | solution.py:139
  30.7 0.0 collective-permute-start.5
  30.7 0.2 collective-permute-done.1
  30.9 2.0 %collective-permute-done.2 = f32[64,128]{1,0:T(8,128)S(1)} collective-permute-done((f32[64,128]{1,0:T(8,128)S(1)}, f32[64,128]{1,0:T(8,128)S(1)}, u32[]{:S(2)}, u32[]{:S(2)}) %collective-permute-start.2) | collective-permute-done | bytes 32800 | tf_op jit(solution)/shard_map/ppermute | solution.py:139
  32.8 0.0 collective-permute-done
  32.8 4.6 %collective-permute-start.3 = (f32[64,128]{1,0:T(8,128)S(1)}, f32[64,128]{1,0:T(8,128)S(1)}, u32[]{:S(2)}, u32[]{:S(2)}) collective-permute-start(f32[64,128]{1,0:T(8,128)S(1)} %fusion.1), channel_id=1, source_target_pairs={{0,12},{2,14},{4,8},{6,10},{8,4},{10,6},{12,0},{14,2},{1,13},{3,15... | collective-permute-start | bytes 98312 | tf_op jit(solution)/shard_map/ppermute | solution.py:139
  37.5 0.0 copy-start
  37.5 0.0 copy-start.1
  37.5 0.0 copy-start.2
  37.5 2.0 %copy.11 = f32[1,1,8192,128]{3,2,1,0:T(8,128)} copy(f32[1,1,8192,128]{3,2,1,0:T(8,128)S(1)} %get-tuple-element.28) | data formatting | bytes 8388608
  39.5 0.0 collective-permute-done.4
  39.5 0.0 collective-permute-done.5
  39.5 0.0 collective-permute-done.3
  39.5 0.0 copy-done
  39.5 0.0 copy-done.1
  39.5 0.0 copy-done.2
  39.5 0.7 %multiply_subtract_fusion = (f32[64,128]{1,0:T(8,128)}, f32[64,128]{1,0:T(8,128)}, f32[64,128]{1,0:T(8,128)}) fusion(f32[64,128]{1,0:T(8,128)S(1)} %copy-done, f32[64,128]{1,0:T(8,128)S(1)} %copy-done.1, f32[64,128]{1,0:T(8,128)S(1)} %copy-done.2, f32[64,128]{1,0:T(8,128)S(1)} %collective-permute-done.5, f32[64,128]{1,0:T(8,128)S(1)} %collective-permute-done.4, ...), kind=kLoop, calls=%fused_computation.8 | loop fusion | flops 139264 | bytes 360448 | tf_op jit(solution)/shard_map/sub | solution.py:154
  (1 shorter events, 0.0 us)
Async XLA Ops:
  23.8 9.0 %collective-permute-start = (f32[128,128]{1,0:T(8,128)S(1)}, f32[128,128]{1,0:T(8,128)S(1)}, u32[]{:S(2)}, u32[]{:S(2)}) collective-permute-start(f32[128,128]{1,0:T(8,128)S(1)} %get-tuple-element.15), channel_id=1, source_target_pairs={{0,2},{2,0},{4,6},{6,4},{8,10},{10,8},{12,14},{14,12},{1,3},{3,1},... | collective-permute-start | bytes 196616 | tf_op jit(solution)/shard_map/ppermute | solution.py:139
  24.0 6.9 %collective-permute-start.1 = (f32[64,128]{1,0:T(8,128)S(1)}, f32[64,128]{1,0:T(8,128)S(1)}, u32[]{:S(2)}, u32[]{:S(2)}) collective-permute-start(f32[64,128]{1,0:T(8,128)S(1)} %get-tuple-element.17), channel_id=1, source_target_pairs={{0,6},{2,4},{4,2},{6,0},{8,14},{10,12},{12,10},{14,8},{1,7},{3,5},... | collective-permute-start | bytes 98312 | tf_op jit(solution)/shard_map/ppermute | solution.py:139
  27.7 5.1 %collective-permute-start.2 = (f32[64,128]{1,0:T(8,128)S(1)}, f32[64,128]{1,0:T(8,128)S(1)}, u32[]{:S(2)}, u32[]{:S(2)}) collective-permute-start(f32[64,128]{1,0:T(8,128)S(1)} %get-tuple-element.18), channel_id=1, source_target_pairs={{0,4},{2,6},{4,0},{6,2},{8,12},{10,14},{12,8},{14,10},{1,5},{3,7},... | collective-permute-start | bytes 98312 | tf_op jit(solution)/shard_map/ppermute | solution.py:139
  28.3 11.2 %collective-permute-start.4 = (f32[64,128]{1,0:T(8,128)S(1)}, f32[64,128]{1,0:T(8,128)S(1)}, u32[]{:S(2)}, u32[]{:S(2)}) collective-permute-start(f32[64,128]{1,0:T(8,128)S(1)} %get-tuple-element.19), channel_id=1, source_target_pairs={{0,4},{2,6},{4,0},{6,2},{8,12},{10,14},{12,8},{14,10},{1,5},{3,7},... | collective-permute-start | bytes 98312 | tf_op jit(solution)/shard_map/ppermute | solution.py:139
  30.7 8.8 %collective-permute-start.5 = (f32[64,128]{1,0:T(8,128)S(1)}, f32[64,128]{1,0:T(8,128)S(1)}, u32[]{:S(2)}, u32[]{:S(2)}) collective-permute-start(f32[64,128]{1,0:T(8,128)S(1)} %get-tuple-element.20), channel_id=1, source_target_pairs={{0,6},{2,4},{4,2},{6,0},{8,14},{10,12},{12,10},{14,8},{1,7},{3,5},... | collective-permute-start | bytes 98312 | tf_op jit(solution)/shard_map/ppermute | solution.py:139
  32.8 6.7 %collective-permute-start.3 = (f32[64,128]{1,0:T(8,128)S(1)}, f32[64,128]{1,0:T(8,128)S(1)}, u32[]{:S(2)}, u32[]{:S(2)}) collective-permute-start(f32[64,128]{1,0:T(8,128)S(1)} %fusion.1), channel_id=1, source_target_pairs={{0,12},{2,14},{4,8},{6,10},{8,4},{10,6},{12,0},{14,2},{1,13},{3,15... | collective-permute-start | bytes 98312 | tf_op jit(solution)/shard_map/ppermute | solution.py:139
  37.5 2.0 %copy-start = (f32[64,128]{1,0:T(8,128)S(1)}, f32[64,128]{1,0:T(8,128)}, u32[]{:S(2)}) copy-start(f32[64,128]{1,0:T(8,128)} %param.11) | copy-start | bytes 98308
  37.5 2.0 %copy-start.1 = (f32[64,128]{1,0:T(8,128)S(1)}, f32[64,128]{1,0:T(8,128)}, u32[]{:S(2)}) copy-start(f32[64,128]{1,0:T(8,128)} %param.13) | copy-start | bytes 98308
  37.5 2.0 %copy-start.2 = (f32[64,128]{1,0:T(8,128)S(1)}, f32[64,128]{1,0:T(8,128)}, u32[]{:S(2)}) copy-start(f32[64,128]{1,0:T(8,128)} %param.12) | copy-start | bytes 98308

commit v5 on v4

--- a/solution.py
+++ b/solution.py
@@ -19,11 +19,12 @@
     return jnp.where(row == ids, 1.0, 0.0).astype(jnp.bfloat16)
 
 
-def pack_kernel(chunks, counts_in, picked_in, gradient, feedback, tiles, new_feedback, near, counts, picked, sems):
+def pack_kernel(chunks, counts_in, picked_in, gradient, feedback, tiles, new_feedback, near, counts, picked, hot, sems):
     owners, slots = picked.shape[2:]
     blocks, width = near.shape
     rows = blocks // owners
     step_rows = blocks // chunks
+    pairs = owners // chunks // 2
 
     def copies(chunk):
         here = pl.ds(pl.multiple_of(chunk * step_rows, step_rows), step_rows)
@@ -43,26 +44,41 @@
             copy.start()
     for copy in lists:
         copy.wait()
-    slot = lax.broadcasted_iota(jnp.int32, (1, slots), 1)
+    lane = lax.broadcasted_iota(jnp.int32, (1, 2 * slots), 1)
+    wide = (tiles.shape[1] - slots, 2 * slots)
+    lower = lax.broadcasted_iota(jnp.int32, wide, 1) < slots
+
+    def prepare(pair, carry):
+        first, second = 2 * pair, 2 * pair + 1
+        ids = jnp.concatenate([picked[0, 0, pl.ds(first, 1), :], picked[0, 0, pl.ds(second, 1), :]], axis=1)
+        limit = jnp.where(lane < slots, counts[0, 0, first], counts[0, 0, second] + slots)
+        ids = jnp.where(lane < limit, ids, -1)
+        hot[pair] = one_hot(rows, ids)
+        sent = jnp.broadcast_to(ids.astype(jnp.float32), wide)
+        turned = pltpu.roll(sent, slots, 1)
+        tiles[first, slots:, :] = jnp.where(lower, sent, turned)
+        tiles[second, slots:, :] = jnp.where(lower, turned, sent)
+        return carry
+
+    lax.fori_loop(0, owners // 2, prepare, 0, unroll=4)
+    lower = lax.broadcasted_iota(jnp.int32, (2 * slots, width), 0) < slots
+    ones = (jnp.where(lower, 1.0, 0.0).astype(jnp.bfloat16), jnp.where(lower, 0.0, 1.0).astype(jnp.bfloat16))
 
     def step(chunk, carry):
         for copy in copies(chunk):
             copy.wait()
-        for part in range(owners // chunks):
-            owner = chunk * (owners // chunks) + part
+        for part in range(2 * pairs):
+            pair, side = chunk * pairs + part // 2, part % 2
+            owner = 2 * pair + side
             here = pl.ds(pl.multiple_of(owner * rows, rows), rows)
             compensated = near[here, :].astype(jnp.float32) + new_feedback[0, 0, here, :]
-            ids = jnp.where(slot < counts[0, 0, owner], picked[0, 0, pl.ds(owner, 1), :], -1)
-            hot = one_hot(rows, ids)
-            named = jnp.dot(hot, jnp.ones((slots, width), jnp.bfloat16), preferred_element_type=jnp.float32)
+            both = hot[pair]
+            named = jnp.dot(both, ones[side], preferred_element_type=jnp.float32)
             new_feedback[0, 0, here, :] = jnp.where(named > 0.0, 0.0, compensated)
             halves = lax.dot_general(
-                hot, split(compensated), (((0,), (0,)), ((), ())), preferred_element_type=jnp.float32
-            )
+                both, split(compensated), (((0,), (0,)), ((), ())), preferred_element_type=jnp.float32
+            )[side * slots : (side + 1) * slots]
             tiles[owner, :slots, :] = halves[:, :width] + halves[:, width:]
-            sent = ids.astype(jnp.float32)
-            sent = jnp.concatenate([sent, sent], axis=1)
-            tiles[owner, slots:, :] = jnp.broadcast_to(sent, (tiles.shape[1] - slots, width))
         return carry
 
     lax.fori_loop(0, chunks, step, 0)
@@ -85,6 +101,7 @@
             pltpu.VMEM((blocks, width), jnp.bfloat16),
             pltpu.SMEM(counts.shape, jnp.int32),
             pltpu.VMEM(picked.shape, jnp.int32),
+            pltpu.VMEM((owners // 2, blocks // owners, 2 * slots), jnp.bfloat16),
             pltpu.SemaphoreType.DMA((3, chunks)),
         ],
         compiler_params=pltpu.CompilerParams(vmem_limit_bytes=32 * 2**20),

time: 40.3 us -> 40.2 us (level)
  no operation moved by 1% of the time
where the time goes in v5:
time: 40.2 us; the launch traced here: 40 us
  blocking collectives  19.1 us (48%)
  starting transfers between devices  11.5 us (29%)
  Pallas kernels  3.96 us (10%)
  waiting for transfers between devices  2.17 us (5%)
  local copies, waits for them, and re-layouts  2.02 us (5%)
  between operations  0.68 us (2%)
  other arithmetic  0.67 us (2%)
    all_to_all x1, blocking collectives, body(): lax.all_to_all(tiles, 'region', split_axis=0, concat_axis=0, tiled=True)  19.1 us
    ppermute x6, starting transfers between devices, swapped(): lax.ppermute(value, 'replica', [(source, source ^ mask) for source in ran...  11.5 us
    pallas_call x1, Pallas kernels, pack(): pl.pallas_call(functools.partial(pack_kernel, chunks), in_specs=[pl.Block...  3.39 us
    ppermute x6, waiting for transfers between devices, swapped(): lax.ppermute(value, 'replica', [(source, source ^ mask) for source in ran...  2.17 us
    unnamed x7, local copies, waits for them, and re-layouts  2.02 us
  transfers between devices with their start and end apart: 6, of which 2 were waited for; matrix products, arithmetic and copies ran while one was open for 5% of the time, Pallas kernels for 0%

profile of v5, /device:TPU:32, one launch (start us, length us, event | category | flops | bytes accessed | tf_op | source)
XLA Modules:
  0.0 40.0 jit_solution(4584855391815091845)
XLA Ops:
  0.6 3.4 %pack.1 = (f32[16,72,128]{2,1,0:T(8,128)S(1)}, f32[1,1,8192,128]{3,2,1,0:T(8,128)S(1)}) custom-call(s32[1,1,16]{2,1,0:T(1,128)} %counts_in.1, s32[1,1,16,64]{3,2,1,0:T(8,128)} %picked_in.1, bf16[1,1,8192,128]{3,2,1,0:T(8,128)(2,1)} %gradient.1, f32[1,1,8192,128]{3,2,1,0:T(8,128)} %feedback.1), custom_call_target="tpu_custom_call" | custom-call | tf_op jit(solution)/shard_map/pack/pallas_call | solution.py:92
  4.0 19.1 %all_to_all.5.got = f32[16,72,128]{2,1,0:T(8,128)S(1)} all-to-all(f32[16,72,128]{2,1,0:T(8,128)S(1)} %get-tuple-element.13), channel_id=1, replica_groups=mesh['region'=16,'replica'=8,'tensor'=2] {'region'}, dimensions={0} | all-to-all | bytes 1179648 | tf_op jit(solution)/shard_map/all_to_all | solution.py:163
  23.1 0.6 %gather_sum.1 = (f32[64,128]{1,0:T(8,128)S(1)}, f32[128,128]{1,0:T(8,128)S(1)}, f32[64,128]{1,0:T(8,128)S(1)}, f32[64,128]{1,0:T(8,128)S(1)}, f32[64,128]{1,0:T(...) custom-call(f32[16,72,128]{2,1,0:T(8,128)S(1)} %all_to_all.5.got), custom_call_target="tpu_custom_call" | custom-call | tf_op jit(solution)/shard_map/gather_sum/pallas_call | solution.py:141
  23.7 0.2 collective-permute-start
  23.8 3.8 %collective-permute-start.1 = (f32[64,128]{1,0:T(8,128)S(1)}, f32[64,128]{1,0:T(8,128)S(1)}, u32[]{:S(2)}, u32[]{:S(2)}) collective-permute-start(f32[64,128]{1,0:T(8,128)S(1)} %get-tuple-element.17), channel_id=1, source_target_pairs={{0,6},{2,4},{4,2},{6,0},{8,14},{10,12},{12,10},{14,8},{1,7},{3,5},... | collective-permute-start | bytes 98312 | tf_op jit(solution)/shard_map/ppermute | solution.py:156
  27.6 0.5 %collective-permute-start.2 = (f32[64,128]{1,0:T(8,128)S(1)}, f32[64,128]{1,0:T(8,128)S(1)}, u32[]{:S(2)}, u32[]{:S(2)}) collective-permute-start(f32[64,128]{1,0:T(8,128)S(1)} %get-tuple-element.18), channel_id=1, source_target_pairs={{0,4},{2,6},{4,0},{6,2},{8,12},{10,14},{12,8},{14,10},{1,5},{3,7},... | collective-permute-start | bytes 98312 | tf_op jit(solution)/shard_map/ppermute | solution.py:156
  28.1 2.4 %collective-permute-start.4 = (f32[64,128]{1,0:T(8,128)S(1)}, f32[64,128]{1,0:T(8,128)S(1)}, u32[]{:S(2)}, u32[]{:S(2)}) collective-permute-start(f32[64,128]{1,0:T(8,128)S(1)} %get-tuple-element.19), channel_id=1, source_target_pairs={{0,4},{2,6},{4,0},{6,2},{8,12},{10,14},{12,8},{14,10},{1,5},{3,7},... | collective-permute-start | bytes 98312 | tf_op jit(solution)/shard_map/ppermute | solution.py:156
  30.5 0.0 collective-permute-start.5
  30.5 0.2 collective-permute-done.1
  30.7 2.0 %collective-permute-done.2 = f32[64,128]{1,0:T(8,128)S(1)} collective-permute-done((f32[64,128]{1,0:T(8,128)S(1)}, f32[64,128]{1,0:T(8,128)S(1)}, u32[]{:S(2)}, u32[]{:S(2)}) %collective-permute-start.2) | collective-permute-done | bytes 32800 | tf_op jit(solution)/shard_map/ppermute | solution.py:156
  32.7 0.0 collective-permute-done
  32.7 4.6 %collective-permute-start.3 = (f32[64,128]{1,0:T(8,128)S(1)}, f32[64,128]{1,0:T(8,128)S(1)}, u32[]{:S(2)}, u32[]{:S(2)}) collective-permute-start(f32[64,128]{1,0:T(8,128)S(1)} %fusion.1), channel_id=1, source_target_pairs={{0,12},{2,14},{4,8},{6,10},{8,4},{10,6},{12,0},{14,2},{1,13},{3,15... | collective-permute-start | bytes 98312 | tf_op jit(solution)/shard_map/ppermute | solution.py:156
  37.3 0.0 copy-start
  37.3 0.0 copy-start.1
  37.3 0.0 copy-start.2
  37.3 2.0 %copy.11 = f32[1,1,8192,128]{3,2,1,0:T(8,128)} copy(f32[1,1,8192,128]{3,2,1,0:T(8,128)S(1)} %get-tuple-element.28) | data formatting | bytes 8388608
  39.3 0.0 collective-permute-done.4
  39.3 0.0 collective-permute-done.5
  39.4 0.0 collective-permute-done.3
  39.4 0.0 copy-done
  39.4 0.0 copy-done.1
  39.4 0.0 copy-done.2
  39.4 0.7 %multiply_subtract_fusion = (f32[64,128]{1,0:T(8,128)}, f32[64,128]{1,0:T(8,128)}, f32[64,128]{1,0:T(8,128)}) fusion(f32[64,128]{1,0:T(8,128)S(1)} %copy-done, f32[64,128]{1,0:T(8,128)S(1)} %copy-done.1, f32[64,128]{1,0:T(8,128)S(1)} %copy-done.2, f32[64,128]{1,0:T(8,128)S(1)} %collective-permute-done.5, f32[64,128]{1,0:T(8,128)S(1)} %collective-permute-done.4, ...), kind=kLoop, calls=%fused_computation.8 | loop fusion | flops 139264 | bytes 360448 | tf_op jit(solution)/shard_map/sub | solution.py:171
  (1 shorter events, 0.0 us)
Async XLA Ops:
  23.7 9.0 %collective-permute-start = (f32[128,128]{1,0:T(8,128)S(1)}, f32[128,128]{1,0:T(8,128)S(1)}, u32[]{:S(2)}, u32[]{:S(2)}) collective-permute-start(f32[128,128]{1,0:T(8,128)S(1)} %get-tuple-element.15), channel_id=1, source_target_pairs={{0,2},{2,0},{4,6},{6,4},{8,10},{10,8},{12,14},{14,12},{1,3},{3,1},... | collective-permute-start | bytes 196616 | tf_op jit(solution)/shard_map/ppermute | solution.py:156
  23.8 6.9 %collective-permute-start.1 = (f32[64,128]{1,0:T(8,128)S(1)}, f32[64,128]{1,0:T(8,128)S(1)}, u32[]{:S(2)}, u32[]{:S(2)}) collective-permute-start(f32[64,128]{1,0:T(8,128)S(1)} %get-tuple-element.17), channel_id=1, source_target_pairs={{0,6},{2,4},{4,2},{6,0},{8,14},{10,12},{12,10},{14,8},{1,7},{3,5},... | collective-permute-start | bytes 98312 | tf_op jit(solution)/shard_map/ppermute | solution.py:156
  27.6 5.1 %collective-permute-start.2 = (f32[64,128]{1,0:T(8,128)S(1)}, f32[64,128]{1,0:T(8,128)S(1)}, u32[]{:S(2)}, u32[]{:S(2)}) collective-permute-start(f32[64,128]{1,0:T(8,128)S(1)} %get-tuple-element.18), channel_id=1, source_target_pairs={{0,4},{2,6},{4,0},{6,2},{8,12},{10,14},{12,8},{14,10},{1,5},{3,7},... | collective-permute-start | bytes 98312 | tf_op jit(solution)/shard_map/ppermute | solution.py:156
  28.1 11.2 %collective-permute-start.4 = (f32[64,128]{1,0:T(8,128)S(1)}, f32[64,128]{1,0:T(8,128)S(1)}, u32[]{:S(2)}, u32[]{:S(2)}) collective-permute-start(f32[64,128]{1,0:T(8,128)S(1)} %get-tuple-element.19), channel_id=1, source_target_pairs={{0,4},{2,6},{4,0},{6,2},{8,12},{10,14},{12,8},{14,10},{1,5},{3,7},... | collective-permute-start | bytes 98312 | tf_op jit(solution)/shard_map/ppermute | solution.py:156
  30.5 8.8 %collective-permute-start.5 = (f32[64,128]{1,0:T(8,128)S(1)}, f32[64,128]{1,0:T(8,128)S(1)}, u32[]{:S(2)}, u32[]{:S(2)}) collective-permute-start(f32[64,128]{1,0:T(8,128)S(1)} %get-tuple-element.20), channel_id=1, source_target_pairs={{0,6},{2,4},{4,2},{6,0},{8,14},{10,12},{12,10},{14,8},{1,7},{3,5},... | collective-permute-start | bytes 98312 | tf_op jit(solution)/shard_map/ppermute | solution.py:156
  32.7 6.6 %collective-permute-start.3 = (f32[64,128]{1,0:T(8,128)S(1)}, f32[64,128]{1,0:T(8,128)S(1)}, u32[]{:S(2)}, u32[]{:S(2)}) collective-permute-start(f32[64,128]{1,0:T(8,128)S(1)} %fusion.1), channel_id=1, source_target_pairs={{0,12},{2,14},{4,8},{6,10},{8,4},{10,6},{12,0},{14,2},{1,13},{3,15... | collective-permute-start | bytes 98312 | tf_op jit(solution)/shard_map/ppermute | solution.py:156
  37.3 2.0 %copy-start = (f32[64,128]{1,0:T(8,128)S(1)}, f32[64,128]{1,0:T(8,128)}, u32[]{:S(2)}) copy-start(f32[64,128]{1,0:T(8,128)} %param.11) | copy-start | bytes 98308
  37.3 2.0 %copy-start.1 = (f32[64,128]{1,0:T(8,128)S(1)}, f32[64,128]{1,0:T(8,128)}, u32[]{:S(2)}) copy-start(f32[64,128]{1,0:T(8,128)} %param.13) | copy-start | bytes 98308
  37.3 2.0 %copy-start.2 = (f32[64,128]{1,0:T(8,128)S(1)}, f32[64,128]{1,0:T(8,128)}, u32[]{:S(2)}) copy-start(f32[64,128]{1,0:T(8,128)} %param.12) | copy-start | bytes 98308

commit v6 on v5

--- a/solution.py
+++ b/solution.py
@@ -109,21 +109,23 @@
     )(*arrays)
 
 
-def gather_sum_kernel(slots, blocks, got, hot, parts, *sums):
+def gather_sum_kernel(slots, rows, blocks, got, *sums):
     me = lax.axis_index("replica")
     sources, _, width = got.shape
-    rows = hot.shape[0]
     own_rows = rows // 8
     lane = lax.broadcasted_iota(jnp.int32, (1, 2 * slots), 1)
-    for pair in range(sources // 2):
+
+    def hot(pair):
         first, second = 2 * pair, 2 * pair + 1
         ids = jnp.where(lane < slots, got[first, slots : slots + 1, :], got[second, slots : slots + 1, :])
         ids = ids.astype(jnp.int32)
-        place = jnp.where(ids < 0, -1, ids ^ (me * own_rows))
-        hot[:, pair * 2 * slots : (pair + 1) * 2 * slots] = one_hot(rows, place)
-        for source in (first, second):
-            parts[source * slots : (source + 1) * slots, :] = split(got[source, :slots, :])
-    halves = jnp.dot(hot[...], parts[...], preferred_element_type=jnp.float32)
+        return one_hot(rows, jnp.where(ids < 0, -1, ids ^ (me * own_rows)))
+
+    halves = jnp.zeros((rows, 2 * width), jnp.float32)
+    for pair in range(0, sources // 2, 2):
+        named = jnp.concatenate([hot(pair), hot(pair + 1)], axis=1)
+        parts = [split(got[source, :slots, :]) for source in range(2 * pair, 2 * pair + 4)]
+        halves += jnp.dot(named, jnp.concatenate(parts, axis=0), preferred_element_type=jnp.float32)
     total = halves[:, :width] + halves[:, width:]
     for group, ref in zip(blocks, sums):
         for position, block in enumerate(group):
@@ -132,21 +134,12 @@
 
 
 def gather_sum(got, rows, blocks):
-    sources, _, width = got.shape
-    slots = width // 2
-
-    def kernel(got, *refs):
-        gather_sum_kernel(slots, blocks, got, *refs[-2:], *refs[:-2])
-
+    width = got.shape[2]
     return pl.pallas_call(
-        kernel,
+        functools.partial(gather_sum_kernel, width // 2, rows, blocks),
         in_specs=[pl.BlockSpec(memory_space=pltpu.VMEM)],
         out_specs=[pl.BlockSpec(memory_space=pltpu.VMEM)] * len(blocks),
         out_shape=[pltpu.VMEM((len(group) * rows // 8, width), jnp.float32) for group in blocks],
-        scratch_shapes=[
-            pltpu.VMEM((rows, sources * slots), jnp.bfloat16),
-            pltpu.VMEM((sources * slots, 2 * width), jnp.bfloat16),
-        ],
         compiler_params=pltpu.CompilerParams(vmem_limit_bytes=16 * 2**20),
         name="gather_sum",
     )(got)
@@ -161,11 +154,10 @@
     reg_rows = own_rows * lax.axis_size("replica")
     tiles, new_feedback = pack(counts, picked, gradient, feedback)
     got = lax.all_to_all(tiles, "region", split_axis=0, concat_axis=0, tiled=True)
-    five, near, four, six, two, three, own = gather_sum(got, reg_rows, ((5,), (7, 1), (4,), (6,), (2,), (3,), (0,)))
-    five = swapped(five, 3)
-    near = swapped(near, 1)
-    six = six + five + near[:own_rows] + swapped(four, 2)
-    total = own + near[own_rows:] + swapped(six, 6) + swapped(two, 2) + swapped(three, 3)
+    far, four, seven, six, two, one, own = gather_sum(got, reg_rows, ((5, 3), (4,), (7,), (6,), (2,), (1,), (0,)))
+    far = swapped(far, 3)
+    six = six + far[:own_rows] + swapped(four, 2) + swapped(seven, 1)
+    total = own + far[own_rows:] + swapped(six, 6) + swapped(two, 2) + swapped(one, 1)
     new_moment = 0.9 * moment + 0.1 * total
     new_second = 0.95 * second + 0.05 * total * total
     new_weights = weights - 0.02 * (new_moment / (jnp.sqrt(new_second) + 1e-08) + 0.1 * weights)

time: 40.2 us -> 39.2 us (0.975)
  waiting for transfers between devices: 2.17 us -> 0.34 us
  starting transfers between devices: 11.5 us -> 12.4 us
    ppermute x6, waiting for transfers between devices: 2.17 us -> 0.34 us  [swapped(): lax.ppermute(value, 'replica', [(source, source ^ mask) for source in ran...]
    ppermute x6, starting transfers between devices: 11.5 us -> 12.4 us  [swapped(): lax.ppermute(value, 'replica', [(source, source ^ mask) for source in ran...]
  transfers between devices with their start and end apart: 6 -> 6, of which waited for: 2 -> 1; matrix products, arithmetic and copies ran while one was open for 5% -> 5% of each run, Pallas kernels for 0% -> 0%
where the time goes in v6:
time: 39.2 us; the launch traced here: 39 us
  blocking collectives  19.1 us (49%)
  starting transfers between devices  12.4 us (32%)
  Pallas kernels  3.84 us (10%)
  local copies, waits for them, and re-layouts  2.02 us (5%)
  between operations  0.68 us (2%)
  other arithmetic  0.67 us (2%)
    all_to_all x1, blocking collectives, body(): lax.all_to_all(tiles, 'region', split_axis=0, concat_axis=0, tiled=True)  19.1 us
    ppermute x6, starting transfers between devices, swapped(): lax.ppermute(value, 'replica', [(source, source ^ mask) for source in ran...  12.4 us
    pallas_call x1, Pallas kernels, pack(): pl.pallas_call(functools.partial(pack_kernel, chunks), in_specs=[pl.Block...  3.39 us
    unnamed x7, local copies, waits for them, and re-layouts  2.02 us
  transfers between devices with their start and end apart: 6, of which 1 were waited for; matrix products, arithmetic and copies ran while one was open for 5% of the time, Pallas kernels for 0%

profile of v6, /device:TPU:32, one launch (start us, length us, event | category | flops | bytes accessed | tf_op | source)
XLA Modules:
  0.0 39.0 jit_solution(1313523314014552123)
XLA Ops:
  0.6 3.4 %pack.1 = (f32[16,72,128]{2,1,0:T(8,128)S(1)}, f32[1,1,8192,128]{3,2,1,0:T(8,128)S(1)}) custom-call(s32[1,1,16]{2,1,0:T(1,128)} %counts_in.1, s32[1,1,16,64]{3,2,1,0:T(8,128)} %picked_in.1, bf16[1,1,8192,128]{3,2,1,0:T(8,128)(2,1)} %gradient.1, f32[1,1,8192,128]{3,2,1,0:T(8,128)} %feedback.1), custom_call_target="tpu_custom_call" | custom-call | tf_op jit(solution)/shard_map/pack/pallas_call | solution.py:92
  4.0 19.1 %all_to_all.5.got = f32[16,72,128]{2,1,0:T(8,128)S(1)} all-to-all(f32[16,72,128]{2,1,0:T(8,128)S(1)} %get-tuple-element.13), channel_id=1, replica_groups=mesh['region'=16,'replica'=8,'tensor'=2] {'region'}, dimensions={0} | all-to-all | bytes 1179648 | tf_op jit(solution)/shard_map/all_to_all | solution.py:156
  23.1 0.4 %gather_sum.1 = (f32[128,128]{1,0:T(8,128)S(1)}, f32[64,128]{1,0:T(8,128)S(1)}, f32[64,128]{1,0:T(8,128)S(1)}, f32[64,128]{1,0:T(8,128)S(1)}, f32[64,128]{1,0:T(...) custom-call(f32[16,72,128]{2,1,0:T(8,128)S(1)} %all_to_all.5.got), custom_call_target="tpu_custom_call" | custom-call | tf_op jit(solution)/shard_map/gather_sum/pallas_call | solution.py:138
  23.5 2.0 %collective-permute-start = (f32[128,128]{1,0:T(8,128)S(1)}, f32[128,128]{1,0:T(8,128)S(1)}, u32[]{:S(2)}, u32[]{:S(2)}) collective-permute-start(f32[128,128]{1,0:T(8,128)S(1)} %get-tuple-element.15), channel_id=1, source_target_pairs={{0,6},{2,4},{4,2},{6,0},{8,14},{10,12},{12,10},{14,8},{1,7},{3,5},... | collective-permute-start | bytes 196616 | tf_op jit(solution)/shard_map/ppermute | solution.py:149
  25.5 1.5 %collective-permute-start.1 = (f32[64,128]{1,0:T(8,128)S(1)}, f32[64,128]{1,0:T(8,128)S(1)}, u32[]{:S(2)}, u32[]{:S(2)}) collective-permute-start(f32[64,128]{1,0:T(8,128)S(1)} %get-tuple-element.17), channel_id=1, source_target_pairs={{0,4},{2,6},{4,0},{6,2},{8,12},{10,14},{12,8},{14,10},{1,5},{3,7},... | collective-permute-start | bytes 98312 | tf_op jit(solution)/shard_map/ppermute | solution.py:149
  27.0 1.4 %collective-permute-start.2 = (f32[64,128]{1,0:T(8,128)S(1)}, f32[64,128]{1,0:T(8,128)S(1)}, u32[]{:S(2)}, u32[]{:S(2)}) collective-permute-start(f32[64,128]{1,0:T(8,128)S(1)} %get-tuple-element.18), channel_id=1, source_target_pairs={{0,2},{2,0},{4,6},{6,4},{8,10},{10,8},{12,14},{14,12},{1,3},{3,1},... | collective-permute-start | bytes 98312 | tf_op jit(solution)/shard_map/ppermute | solution.py:149
  28.4 2.9 %collective-permute-start.4 = (f32[64,128]{1,0:T(8,128)S(1)}, f32[64,128]{1,0:T(8,128)S(1)}, u32[]{:S(2)}, u32[]{:S(2)}) collective-permute-start(f32[64,128]{1,0:T(8,128)S(1)} %get-tuple-element.19), channel_id=1, source_target_pairs={{0,4},{2,6},{4,0},{6,2},{8,12},{10,14},{12,8},{14,10},{1,5},{3,7},... | collective-permute-start | bytes 98312 | tf_op jit(solution)/shard_map/ppermute | solution.py:149
  31.3 0.0 collective-permute-start.5
  31.3 0.0 collective-permute-done.1
  31.3 0.3 collective-permute-done.2
  31.6 0.0 collective-permute-done
  31.6 4.7 %collective-permute-start.3 = (f32[64,128]{1,0:T(8,128)S(1)}, f32[64,128]{1,0:T(8,128)S(1)}, u32[]{:S(2)}, u32[]{:S(2)}) collective-permute-start(f32[64,128]{1,0:T(8,128)S(1)} %fusion.2), channel_id=1, source_target_pairs={{0,12},{2,14},{4,8},{6,10},{8,4},{10,6},{12,0},{14,2},{1,13},{3,15... | collective-permute-start | bytes 98312 | tf_op jit(solution)/shard_map/ppermute | solution.py:149
  36.3 0.0 copy-start
  36.3 0.0 copy-start.1
  36.3 0.0 copy-start.2
  36.3 2.0 %copy.11 = f32[1,1,8192,128]{3,2,1,0:T(8,128)} copy(f32[1,1,8192,128]{3,2,1,0:T(8,128)S(1)} %get-tuple-element.28) | data formatting | bytes 8388608
  38.3 0.0 collective-permute-done.4
  38.3 0.0 collective-permute-done.5
  38.3 0.0 collective-permute-done.3
  38.3 0.0 copy-done
  38.3 0.0 copy-done.1
  38.4 0.0 copy-done.2
  38.4 0.7 %multiply_subtract_fusion = (f32[64,128]{1,0:T(8,128)}, f32[64,128]{1,0:T(8,128)}, f32[64,128]{1,0:T(8,128)}) fusion(f32[64,128]{1,0:T(8,128)S(1)} %copy-done, f32[64,128]{1,0:T(8,128)S(1)} %copy-done.1, f32[64,128]{1,0:T(8,128)S(1)} %copy-done.2, f32[64,128]{1,0:T(8,128)S(1)} %collective-permute-done.5, f32[64,128]{1,0:T(8,128)S(1)} %collective-permute-done.4, ...), kind=kLoop, calls=%fused_computation.9 | loop fusion | flops 139264 | bytes 360448 | tf_op jit(solution)/shard_map/sub | solution.py:163
  (1 shorter events, 0.0 us)
Async XLA Ops:
  23.5 8.1 %collective-permute-start = (f32[128,128]{1,0:T(8,128)S(1)}, f32[128,128]{1,0:T(8,128)S(1)}, u32[]{:S(2)}, u32[]{:S(2)}) collective-permute-start(f32[128,128]{1,0:T(8,128)S(1)} %get-tuple-element.15), channel_id=1, source_target_pairs={{0,6},{2,4},{4,2},{6,0},{8,14},{10,12},{12,10},{14,8},{1,7},{3,5},... | collective-permute-start | bytes 196616 | tf_op jit(solution)/shard_map/ppermute | solution.py:149
  25.5 5.7 %collective-permute-start.1 = (f32[64,128]{1,0:T(8,128)S(1)}, f32[64,128]{1,0:T(8,128)S(1)}, u32[]{:S(2)}, u32[]{:S(2)}) collective-permute-start(f32[64,128]{1,0:T(8,128)S(1)} %get-tuple-element.17), channel_id=1, source_target_pairs={{0,4},{2,6},{4,0},{6,2},{8,12},{10,14},{12,8},{14,10},{1,5},{3,7},... | collective-permute-start | bytes 98312 | tf_op jit(solution)/shard_map/ppermute | solution.py:149
  27.0 4.6 %collective-permute-start.2 = (f32[64,128]{1,0:T(8,128)S(1)}, f32[64,128]{1,0:T(8,128)S(1)}, u32[]{:S(2)}, u32[]{:S(2)}) collective-permute-start(f32[64,128]{1,0:T(8,128)S(1)} %get-tuple-element.18), channel_id=1, source_target_pairs={{0,2},{2,0},{4,6},{6,4},{8,10},{10,8},{12,14},{14,12},{1,3},{3,1},... | collective-permute-start | bytes 98312 | tf_op jit(solution)/shard_map/ppermute | solution.py:149
  28.4 9.9 %collective-permute-start.4 = (f32[64,128]{1,0:T(8,128)S(1)}, f32[64,128]{1,0:T(8,128)S(1)}, u32[]{:S(2)}, u32[]{:S(2)}) collective-permute-start(f32[64,128]{1,0:T(8,128)S(1)} %get-tuple-element.19), channel_id=1, source_target_pairs={{0,4},{2,6},{4,0},{6,2},{8,12},{10,14},{12,8},{14,10},{1,5},{3,7},... | collective-permute-start | bytes 98312 | tf_op jit(solution)/shard_map/ppermute | solution.py:149
  31.3 7.0 %collective-permute-start.5 = (f32[64,128]{1,0:T(8,128)S(1)}, f32[64,128]{1,0:T(8,128)S(1)}, u32[]{:S(2)}, u32[]{:S(2)}) collective-permute-start(f32[64,128]{1,0:T(8,128)S(1)} %get-tuple-element.20), channel_id=1, source_target_pairs={{0,2},{2,0},{4,6},{6,4},{8,10},{10,8},{12,14},{14,12},{1,3},{3,1},... | collective-permute-start | bytes 98312 | tf_op jit(solution)/shard_map/ppermute | solution.py:149
  31.6 6.7 %collective-permute-start.3 = (f32[64,128]{1,0:T(8,128)S(1)}, f32[64,128]{1,0:T(8,128)S(1)}, u32[]{:S(2)}, u32[]{:S(2)}) collective-permute-start(f32[64,128]{1,0:T(8,128)S(1)} %fusion.2), channel_id=1, source_target_pairs={{0,12},{2,14},{4,8},{6,10},{8,4},{10,6},{12,0},{14,2},{1,13},{3,15... | collective-permute-start | bytes 98312 | tf_op jit(solution)/shard_map/ppermute | solution.py:149
  36.3 2.0 %copy-start = (f32[64,128]{1,0:T(8,128)S(1)}, f32[64,128]{1,0:T(8,128)}, u32[]{:S(2)}) copy-start(f32[64,128]{1,0:T(8,128)} %param.11) | copy-start | bytes 98308
  36.3 2.0 %copy-start.1 = (f32[64,128]{1,0:T(8,128)S(1)}, f32[64,128]{1,0:T(8,128)}, u32[]{:S(2)}) copy-start(f32[64,128]{1,0:T(8,128)} %param.13) | copy-start | bytes 98308
  36.3 2.0 %copy-start.2 = (f32[64,128]{1,0:T(8,128)S(1)}, f32[64,128]{1,0:T(8,128)}, u32[]{:S(2)}) copy-start(f32[64,128]{1,0:T(8,128)} %param.12) | copy-start | bytes 98308

commit v7 on v6

--- a/solution.py
+++ b/solution.py
@@ -45,7 +45,7 @@
     for copy in lists:
         copy.wait()
     lane = lax.broadcasted_iota(jnp.int32, (1, 2 * slots), 1)
-    wide = (tiles.shape[1] - slots, 2 * slots)
+    wide = (8, 2 * slots)
     lower = lax.broadcasted_iota(jnp.int32, wide, 1) < slots
 
     def prepare(pair, carry):
@@ -56,8 +56,8 @@
         hot[pair] = one_hot(rows, ids)
         sent = jnp.broadcast_to(ids.astype(jnp.float32), wide)
         turned = pltpu.roll(sent, slots, 1)
-        tiles[first, slots:, :] = jnp.where(lower, sent, turned)
-        tiles[second, slots:, :] = jnp.where(lower, turned, sent)
+        tiles[pl.ds(first * (slots + 1) + slots, 1), :] = jnp.where(lower, sent, turned)[:1]
+        tiles[pl.ds(second * (slots + 1) + slots, 1), :] = jnp.where(lower, turned, sent)[:1]
         return carry
 
     lax.fori_loop(0, owners // 2, prepare, 0, unroll=4)
@@ -78,7 +78,7 @@
             halves = lax.dot_general(
                 both, split(compensated), (((0,), (0,)), ((), ())), preferred_element_type=jnp.float32
             )[side * slots : (side + 1) * slots]
-            tiles[owner, :slots, :] = halves[:, :width] + halves[:, width:]
+            tiles[pl.ds(owner * (slots + 1), slots), :] = halves[:, :width] + halves[:, width:]
         return carry
 
     lax.fori_loop(0, chunks, step, 0)
@@ -94,7 +94,7 @@
         in_specs=[pl.BlockSpec(memory_space=pltpu.HBM)] * 4,
         out_specs=[pl.BlockSpec(memory_space=pltpu.VMEM)] * 2,
         out_shape=[
-            pltpu.VMEM((owners, slots + 8, width), jnp.float32),
+            pltpu.VMEM((owners * (slots + 1), width), jnp.float32),
             pltpu.VMEM(feedback.shape, jnp.float32),
         ],
         scratch_shapes=[
@@ -111,20 +111,26 @@
 
 def gather_sum_kernel(slots, rows, blocks, got, *sums):
     me = lax.axis_index("replica")
-    sources, _, width = got.shape
+    width = got.shape[1]
+    sources = got.shape[0] // (slots + 1)
     own_rows = rows // 8
     lane = lax.broadcasted_iota(jnp.int32, (1, 2 * slots), 1)
 
+    def numbers(source):
+        return got[(source + 1) * (slots + 1) - 1 : (source + 1) * (slots + 1), :]
+
+    def tile(source):
+        return got[source * (slots + 1) : (source + 1) * (slots + 1) - 1, :]
+
     def hot(pair):
         first, second = 2 * pair, 2 * pair + 1
-        ids = jnp.where(lane < slots, got[first, slots : slots + 1, :], got[second, slots : slots + 1, :])
-        ids = ids.astype(jnp.int32)
+        ids = jnp.where(lane < slots, numbers(first), numbers(second)).astype(jnp.int32)
         return one_hot(rows, jnp.where(ids < 0, -1, ids ^ (me * own_rows)))
 
     halves = jnp.zeros((rows, 2 * width), jnp.float32)
     for pair in range(0, sources // 2, 2):
         named = jnp.concatenate([hot(pair), hot(pair + 1)], axis=1)
-        parts = [split(got[source, :slots, :]) for source in range(2 * pair, 2 * pair + 4)]
+        parts = [split(tile(source)) for source in range(2 * pair, 2 * pair + 4)]
         halves += jnp.dot(named, jnp.concatenate(parts, axis=0), preferred_element_type=jnp.float32)
     total = halves[:, :width] + halves[:, width:]
     for group, ref in zip(blocks, sums):
@@ -133,16 +139,16 @@
             ref[here, :] = total[block * own_rows : (block + 1) * own_rows]
 
 
-def gather_sum(got, rows, blocks):
-    width = got.shape[2]
+def gather_sum(got, slots, rows, blocks):
+    width = got.shape[1]
     return pl.pallas_call(
-        functools.partial(gather_sum_kernel, width // 2, rows, blocks),
+        functools.partial(gather_sum_kernel, slots, rows, blocks),
         in_specs=[pl.BlockSpec(memory_space=pltpu.VMEM)],
         out_specs=[pl.BlockSpec(memory_space=pltpu.VMEM)] * len(blocks),
         out_shape=[pltpu.VMEM((len(group) * rows // 8, width), jnp.float32) for group in blocks],
         compiler_params=pltpu.CompilerParams(vmem_limit_bytes=16 * 2**20),
         name="gather_sum",
-    )(got)
+    )(pltpu.with_memory_space_constraint(got, pltpu.VMEM))
 
 
 def swapped(value, mask):
@@ -153,11 +159,15 @@
     own_rows = weights.shape[0]
     reg_rows = own_rows * lax.axis_size("replica")
     tiles, new_feedback = pack(counts, picked, gradient, feedback)
-    got = lax.all_to_all(tiles, "region", split_axis=0, concat_axis=0, tiled=True)
-    far, four, seven, six, two, one, own = gather_sum(got, reg_rows, ((5, 3), (4,), (7,), (6,), (2,), (1,), (0,)))
+    rows, width = tiles.shape
+    got = lax.all_to_all(tiles.reshape(rows, 1, width), "region", split_axis=0, concat_axis=0, tiled=True)
+    got = got.reshape(rows, width)
+    far, four, seven, six, one, two, own = gather_sum(
+        got, picked.shape[3], reg_rows, ((5, 3), (4,), (7,), (6,), (1,), (2,), (0,))
+    )
     far = swapped(far, 3)
     six = six + far[:own_rows] + swapped(four, 2) + swapped(seven, 1)
-    total = own + far[own_rows:] + swapped(six, 6) + swapped(two, 2) + swapped(one, 1)
+    total = own + far[own_rows:] + swapped(six, 6) + swapped(one, 1) + swapped(two, 2)
     new_moment = 0.9 * moment + 0.1 * total
     new_second = 0.95 * second + 0.05 * total * total
     new_weights = weights - 0.02 * (new_moment / (jnp.sqrt(new_second) + 1e-08) + 0.1 * weights)

time: 39.2 us -> 39.1 us (level)
  starting transfers between devices: 12.4 us -> 13.1 us
  blocking collectives: 19.1 us -> 18.6 us
    ppermute x6, starting transfers between devices: 12.4 us -> 13.1 us  [swapped(): lax.ppermute(value, 'replica', [(source, source ^ mask) for source in ran...]
    all_to_all x1, blocking collectives: 19.1 us -> 18.6 us  [body(): lax.all_to_all(tiles.reshape(rows, 1, width), 'region', split_axis=0, con...]
  transfers between devices with their start and end apart: 6 -> 6, of which waited for: 1 -> 0; matrix products, arithmetic and copies ran while one was open for 5% -> 5% of each run, Pallas kernels for 0% -> 0%
where the time goes in v7:
time: 39.1 us; the launch traced here: 39 us
  blocking collectives  18.6 us (48%)
  starting transfers between devices  13.1 us (34%)
  Pallas kernels  3.84 us (10%)
  local copies, waits for them, and re-layouts  2.02 us (5%)
  between operations  0.69 us (2%)
  other arithmetic  0.67 us (2%)
    all_to_all x1, blocking collectives, body(): lax.all_to_all(tiles.reshape(rows, 1, width), 'region', split_axis=0, con...  18.6 us
    ppermute x6, starting transfers between devices, swapped(): lax.ppermute(value, 'replica', [(source, source ^ mask) for source in ran...  13.1 us
    pallas_call x1, Pallas kernels, pack(): pl.pallas_call(functools.partial(pack_kernel, chunks), in_specs=[pl.Block...  3.4 us
    unnamed x7, local copies, waits for them, and re-layouts  2.02 us
  transfers between devices with their start and end apart: 6, of which 0 were waited for; matrix products, arithmetic and copies ran while one was open for 5% of the time, Pallas kernels for 0%

profile of v7, /device:TPU:32, one launch (start us, length us, event | category | flops | bytes accessed | tf_op | source)
XLA Modules:
  0.0 39.0 jit_solution(1906603934331358481)
XLA Ops:
  0.6 3.4 %pack.1 = (f32[1040,128]{1,0:T(8,128)S(1)}, f32[1,1,8192,128]{3,2,1,0:T(8,128)S(1)}) custom-call(s32[1,1,16]{2,1,0:T(1,128)} %counts_in.1, s32[1,1,16,64]{3,2,1,0:T(8,128)} %picked_in.1, bf16[1,1,8192,128]{3,2,1,0:T(8,128)(2,1)} %gradient.1, f32[1,1,8192,128]{3,2,1,0:T(8,128)} %feedback.1), custom_call_target="tpu_custom_call" | custom-call | tf_op jit(solution)/shard_map/pack/pallas_call | solution.py:92
  4.0 18.6 %all_to_all.5 = f32[1040,1,128]{2,1,0:T(1,128)S(1)} all-to-all(f32[1040,1,128]{2,1,0:T(1,128)S(1)} %bitcast.5), channel_id=1, replica_groups=mesh['region'=16,'replica'=8,'tensor'=2] {'region'}, dimensions={0} | all-to-all | bytes 1064960 | tf_op jit(solution)/shard_map/all_to_all | solution.py:163
  22.7 0.4 %gather_sum.1 = (f32[128,128]{1,0:T(8,128)S(1)}, f32[64,128]{1,0:T(8,128)S(1)}, f32[64,128]{1,0:T(8,128)S(1)}, f32[64,128]{1,0:T(8,128)S(1)}, f32[64,128]{1,0:T(...) custom-call(f32[1040,128]{1,0:T(8,128)S(1)} %bitcast.4), custom_call_target="tpu_custom_call" | custom-call | tf_op jit(solution)/shard_map/gather_sum/pallas_call | solution.py:144
  23.1 2.0 %collective-permute-start = (f32[128,128]{1,0:T(8,128)S(1)}, f32[128,128]{1,0:T(8,128)S(1)}, u32[]{:S(2)}, u32[]{:S(2)}) collective-permute-start(f32[128,128]{1,0:T(8,128)S(1)} %get-tuple-element.15), channel_id=1, source_target_pairs={{0,6},{2,4},{4,2},{6,0},{8,14},{10,12},{12,10},{14,8},{1,7},{3,5},... | collective-permute-start | bytes 196616 | tf_op jit(solution)/shard_map/ppermute | solution.py:155
  25.1 1.5 %collective-permute-start.1 = (f32[64,128]{1,0:T(8,128)S(1)}, f32[64,128]{1,0:T(8,128)S(1)}, u32[]{:S(2)}, u32[]{:S(2)}) collective-permute-start(f32[64,128]{1,0:T(8,128)S(1)} %get-tuple-element.17), channel_id=1, source_target_pairs={{0,4},{2,6},{4,0},{6,2},{8,12},{10,14},{12,8},{14,10},{1,5},{3,7},... | collective-permute-start | bytes 98312 | tf_op jit(solution)/shard_map/ppermute | solution.py:155
  26.6 1.4 %collective-permute-start.2 = (f32[64,128]{1,0:T(8,128)S(1)}, f32[64,128]{1,0:T(8,128)S(1)}, u32[]{:S(2)}, u32[]{:S(2)}) collective-permute-start(f32[64,128]{1,0:T(8,128)S(1)} %get-tuple-element.18), channel_id=1, source_target_pairs={{0,2},{2,0},{4,6},{6,4},{8,10},{10,8},{12,14},{14,12},{1,3},{3,1},... | collective-permute-start | bytes 98312 | tf_op jit(solution)/shard_map/ppermute | solution.py:155
  28.0 0.7 %collective-permute-start.4 = (f32[64,128]{1,0:T(8,128)S(1)}, f32[64,128]{1,0:T(8,128)S(1)}, u32[]{:S(2)}, u32[]{:S(2)}) collective-permute-start(f32[64,128]{1,0:T(8,128)S(1)} %get-tuple-element.19), channel_id=1, source_target_pairs={{0,2},{2,0},{4,6},{6,4},{8,10},{10,8},{12,14},{14,12},{1,3},{3,1},... | collective-permute-start | bytes 98312 | tf_op jit(solution)/shard_map/ppermute | solution.py:155
  28.6 2.3 %collective-permute-start.5 = (f32[64,128]{1,0:T(8,128)S(1)}, f32[64,128]{1,0:T(8,128)S(1)}, u32[]{:S(2)}, u32[]{:S(2)}) collective-permute-start(f32[64,128]{1,0:T(8,128)S(1)} %get-tuple-element.20), channel_id=1, source_target_pairs={{0,4},{2,6},{4,0},{6,2},{8,12},{10,14},{12,8},{14,10},{1,5},{3,7},... | collective-permute-start | bytes 98312 | tf_op jit(solution)/shard_map/ppermute | solution.py:155
  30.9 0.0 collective-permute-done.1
  30.9 0.0 collective-permute-done.2
  30.9 0.0 collective-permute-done
  30.9 5.4 %collective-permute-start.3 = (f32[64,128]{1,0:T(8,128)S(1)}, f32[64,128]{1,0:T(8,128)S(1)}, u32[]{:S(2)}, u32[]{:S(2)}) collective-permute-start(f32[64,128]{1,0:T(8,128)S(1)} %fusion.2), channel_id=1, source_target_pairs={{0,12},{2,14},{4,8},{6,10},{8,4},{10,6},{12,0},{14,2},{1,13},{3,15... | collective-permute-start | bytes 98312 | tf_op jit(solution)/shard_map/ppermute | solution.py:155
  36.3 0.0 copy-start
  36.3 0.0 copy-start.1
  36.3 0.0 copy-start.2
  36.3 2.0 %copy.12 = f32[1,1,8192,128]{3,2,1,0:T(8,128)} copy(f32[1,1,8192,128]{3,2,1,0:T(8,128)S(1)} %get-tuple-element.28) | data formatting | bytes 8388608
  38.3 0.0 collective-permute-done.4
  38.3 0.0 collective-permute-done.5
  38.3 0.0 collective-permute-done.3
  38.3 0.0 copy-done
  38.3 0.0 copy-done.1
  38.3 0.0 copy-done.2
  38.4 0.7 %multiply_subtract_fusion = (f32[64,128]{1,0:T(8,128)}, f32[64,128]{1,0:T(8,128)}, f32[64,128]{1,0:T(8,128)}) fusion(f32[64,128]{1,0:T(8,128)S(1)} %copy-done, f32[64,128]{1,0:T(8,128)S(1)} %copy-done.1, f32[64,128]{1,0:T(8,128)S(1)} %copy-done.2, f32[64,128]{1,0:T(8,128)S(1)} %collective-permute-done.5, f32[64,128]{1,0:T(8,128)S(1)} %collective-permute-done.4, ...), kind=kLoop, calls=%fused_computation.9 | loop fusion | flops 139264 | bytes 360448 | tf_op jit(solution)/shard_map/sub | solution.py:173
  (1 shorter events, 0.0 us)
Async XLA Ops:
  23.1 7.8 %collective-permute-start = (f32[128,128]{1,0:T(8,128)S(1)}, f32[128,128]{1,0:T(8,128)S(1)}, u32[]{:S(2)}, u32[]{:S(2)}) collective-permute-start(f32[128,128]{1,0:T(8,128)S(1)} %get-tuple-element.15), channel_id=1, source_target_pairs={{0,6},{2,4},{4,2},{6,0},{8,14},{10,12},{12,10},{14,8},{1,7},{3,5},... | collective-permute-start | bytes 196616 | tf_op jit(solution)/shard_map/ppermute | solution.py:155
  25.1 5.8 %collective-permute-start.1 = (f32[64,128]{1,0:T(8,128)S(1)}, f32[64,128]{1,0:T(8,128)S(1)}, u32[]{:S(2)}, u32[]{:S(2)}) collective-permute-start(f32[64,128]{1,0:T(8,128)S(1)} %get-tuple-element.17), channel_id=1, source_target_pairs={{0,4},{2,6},{4,0},{6,2},{8,12},{10,14},{12,8},{14,10},{1,5},{3,7},... | collective-permute-start | bytes 98312 | tf_op jit(solution)/shard_map/ppermute | solution.py:155
  26.6 4.3 %collective-permute-start.2 = (f32[64,128]{1,0:T(8,128)S(1)}, f32[64,128]{1,0:T(8,128)S(1)}, u32[]{:S(2)}, u32[]{:S(2)}) collective-permute-start(f32[64,128]{1,0:T(8,128)S(1)} %get-tuple-element.18), channel_id=1, source_target_pairs={{0,2},{2,0},{4,6},{6,4},{8,10},{10,8},{12,14},{14,12},{1,3},{3,1},... | collective-permute-start | bytes 98312 | tf_op jit(solution)/shard_map/ppermute | solution.py:155
  28.0 10.4 %collective-permute-start.4 = (f32[64,128]{1,0:T(8,128)S(1)}, f32[64,128]{1,0:T(8,128)S(1)}, u32[]{:S(2)}, u32[]{:S(2)}) collective-permute-start(f32[64,128]{1,0:T(8,128)S(1)} %get-tuple-element.19), channel_id=1, source_target_pairs={{0,2},{2,0},{4,6},{6,4},{8,10},{10,8},{12,14},{14,12},{1,3},{3,1},... | collective-permute-start | bytes 98312 | tf_op jit(solution)/shard_map/ppermute | solution.py:155
  28.6 9.7 %collective-permute-start.5 = (f32[64,128]{1,0:T(8,128)S(1)}, f32[64,128]{1,0:T(8,128)S(1)}, u32[]{:S(2)}, u32[]{:S(2)}) collective-permute-start(f32[64,128]{1,0:T(8,128)S(1)} %get-tuple-element.20), channel_id=1, source_target_pairs={{0,4},{2,6},{4,0},{6,2},{8,12},{10,14},{12,8},{14,10},{1,5},{3,7},... | collective-permute-start | bytes 98312 | tf_op jit(solution)/shard_map/ppermute | solution.py:155
  30.9 7.4 %collective-permute-start.3 = (f32[64,128]{1,0:T(8,128)S(1)}, f32[64,128]{1,0:T(8,128)S(1)}, u32[]{:S(2)}, u32[]{:S(2)}) collective-permute-start(f32[64,128]{1,0:T(8,128)S(1)} %fusion.2), channel_id=1, source_target_pairs={{0,12},{2,14},{4,8},{6,10},{8,4},{10,6},{12,0},{14,2},{1,13},{3,15... | collective-permute-start | bytes 98312 | tf_op jit(solution)/shard_map/ppermute | solution.py:155
  36.3 2.0 %copy-start = (f32[64,128]{1,0:T(8,128)S(1)}, f32[64,128]{1,0:T(8,128)}, u32[]{:S(2)}) copy-start(f32[64,128]{1,0:T(8,128)} %param.11) | copy-start | bytes 98308
  36.3 2.0 %copy-start.1 = (f32[64,128]{1,0:T(8,128)S(1)}, f32[64,128]{1,0:T(8,128)}, u32[]{:S(2)}) copy-start(f32[64,128]{1,0:T(8,128)} %param.13) | copy-start | bytes 98308
  36.3 2.0 %copy-start.2 = (f32[64,128]{1,0:T(8,128)S(1)}, f32[64,128]{1,0:T(8,128)}, u32[]{:S(2)}) copy-start(f32[64,128]{1,0:T(8,128)} %param.12) | copy-start | bytes 98308

commit v8 on v7

--- a/solution.py
+++ b/solution.py
@@ -61,24 +61,27 @@
         return carry
 
     lax.fori_loop(0, owners // 2, prepare, 0, unroll=4)
-    lower = lax.broadcasted_iota(jnp.int32, (2 * slots, width), 0) < slots
-    ones = (jnp.where(lower, 1.0, 0.0).astype(jnp.bfloat16), jnp.where(lower, 0.0, 1.0).astype(jnp.bfloat16))
+    column = lax.broadcasted_iota(jnp.int32, (2 * slots, 2 * width), 1) < width
+    lower = lax.broadcasted_iota(jnp.int32, (2 * slots, 2 * width), 0) < slots
+    ones = jnp.where(lower == column, 1.0, 0.0).astype(jnp.bfloat16)
 
     def step(chunk, carry):
         for copy in copies(chunk):
             copy.wait()
-        for part in range(2 * pairs):
-            pair, side = chunk * pairs + part // 2, part % 2
-            owner = 2 * pair + side
-            here = pl.ds(pl.multiple_of(owner * rows, rows), rows)
-            compensated = near[here, :].astype(jnp.float32) + new_feedback[0, 0, here, :]
+        for part in range(pairs):
+            pair = chunk * pairs + part
             both = hot[pair]
-            named = jnp.dot(both, ones[side], preferred_element_type=jnp.float32)
-            new_feedback[0, 0, here, :] = jnp.where(named > 0.0, 0.0, compensated)
-            halves = lax.dot_general(
-                both, split(compensated), (((0,), (0,)), ((), ())), preferred_element_type=jnp.float32
-            )[side * slots : (side + 1) * slots]
-            tiles[pl.ds(owner * (slots + 1), slots), :] = halves[:, :width] + halves[:, width:]
+            named = jnp.dot(both, ones, preferred_element_type=jnp.float32)
+            for side in (0, 1):
+                owner = 2 * pair + side
+                here = pl.ds(pl.multiple_of(owner * rows, rows), rows)
+                compensated = near[here, :].astype(jnp.float32) + new_feedback[0, 0, here, :]
+                own = named[:, side * width : (side + 1) * width]
+                new_feedback[0, 0, here, :] = jnp.where(own > 0.0, 0.0, compensated)
+                halves = lax.dot_general(
+                    both, split(compensated), (((0,), (0,)), ((), ())), preferred_element_type=jnp.float32
+                )[side * slots : (side + 1) * slots]
+                tiles[pl.ds(owner * (slots + 1), slots), :] = halves[:, :width] + halves[:, width:]
         return carry
 
     lax.fori_loop(0, chunks, step, 0)

time: 39.1 us -> 39.1 us (level)
  no operation moved by 1% of the time
where the time goes in v8:
time: 39.1 us; the launch traced here: 39 us
  blocking collectives  18.6 us (48%)
  starting transfers between devices  13.1 us (34%)
  Pallas kernels  3.84 us (10%)
  local copies, waits for them, and re-layouts  2.02 us (5%)
  between operations  0.69 us (2%)
  other arithmetic  0.67 us (2%)
    all_to_all x1, blocking collectives, body(): lax.all_to_all(tiles.reshape(rows, 1, width), 'region', split_axis=0, con...  18.6 us
    ppermute x6, starting transfers between devices, swapped(): lax.ppermute(value, 'replica', [(source, source ^ mask) for source in ran...  13.1 us
    pallas_call x1, Pallas kernels, pack(): pl.pallas_call(functools.partial(pack_kernel, chunks), in_specs=[pl.Block...  3.4 us
    unnamed x7, local copies, waits for them, and re-layouts  2.02 us
  transfers between devices with their start and end apart: 6, of which 0 were waited for; matrix products, arithmetic and copies ran while one was open for 5% of the time, Pallas kernels for 0%

profile of v8, /device:TPU:32, one launch (start us, length us, event | category | flops | bytes accessed | tf_op | source)
XLA Modules:
  0.0 39.0 jit_solution(9077575384563847632)
XLA Ops:
  0.6 3.4 %pack.1 = (f32[1040,128]{1,0:T(8,128)S(1)}, f32[1,1,8192,128]{3,2,1,0:T(8,128)S(1)}) custom-call(s32[1,1,16]{2,1,0:T(1,128)} %counts_in.1, s32[1,1,16,64]{3,2,1,0:T(8,128)} %picked_in.1, bf16[1,1,8192,128]{3,2,1,0:T(8,128)(2,1)} %gradient.1, f32[1,1,8192,128]{3,2,1,0:T(8,128)} %feedback.1), custom_call_target="tpu_custom_call" | custom-call | tf_op jit(solution)/shard_map/pack/pallas_call | solution.py:95
  4.0 18.6 %all_to_all.5 = f32[1040,1,128]{2,1,0:T(1,128)S(1)} all-to-all(f32[1040,1,128]{2,1,0:T(1,128)S(1)} %bitcast.5), channel_id=1, replica_groups=mesh['region'=16,'replica'=8,'tensor'=2] {'region'}, dimensions={0} | all-to-all | bytes 1064960 | tf_op jit(solution)/shard_map/all_to_all | solution.py:166
  22.7 0.4 %gather_sum.1 = (f32[128,128]{1,0:T(8,128)S(1)}, f32[64,128]{1,0:T(8,128)S(1)}, f32[64,128]{1,0:T(8,128)S(1)}, f32[64,128]{1,0:T(8,128)S(1)}, f32[64,128]{1,0:T(...) custom-call(f32[1040,128]{1,0:T(8,128)S(1)} %bitcast.4), custom_call_target="tpu_custom_call" | custom-call | tf_op jit(solution)/shard_map/gather_sum/pallas_call | solution.py:147
  23.1 2.0 %collective-permute-start = (f32[128,128]{1,0:T(8,128)S(1)}, f32[128,128]{1,0:T(8,128)S(1)}, u32[]{:S(2)}, u32[]{:S(2)}) collective-permute-start(f32[128,128]{1,0:T(8,128)S(1)} %get-tuple-element.15), channel_id=1, source_target_pairs={{0,6},{2,4},{4,2},{6,0},{8,14},{10,12},{12,10},{14,8},{1,7},{3,5},... | collective-permute-start | bytes 196616 | tf_op jit(solution)/shard_map/ppermute | solution.py:158
  25.1 1.5 %collective-permute-start.1 = (f32[64,128]{1,0:T(8,128)S(1)}, f32[64,128]{1,0:T(8,128)S(1)}, u32[]{:S(2)}, u32[]{:S(2)}) collective-permute-start(f32[64,128]{1,0:T(8,128)S(1)} %get-tuple-element.17), channel_id=1, source_target_pairs={{0,4},{2,6},{4,0},{6,2},{8,12},{10,14},{12,8},{14,10},{1,5},{3,7},... | collective-permute-start | bytes 98312 | tf_op jit(solution)/shard_map/ppermute | solution.py:158
  26.6 1.4 %collective-permute-start.2 = (f32[64,128]{1,0:T(8,128)S(1)}, f32[64,128]{1,0:T(8,128)S(1)}, u32[]{:S(2)}, u32[]{:S(2)}) collective-permute-start(f32[64,128]{1,0:T(8,128)S(1)} %get-tuple-element.18), channel_id=1, source_target_pairs={{0,2},{2,0},{4,6},{6,4},{8,10},{10,8},{12,14},{14,12},{1,3},{3,1},... | collective-permute-start | bytes 98312 | tf_op jit(solution)/shard_map/ppermute | solution.py:158
  28.0 0.7 %collective-permute-start.4 = (f32[64,128]{1,0:T(8,128)S(1)}, f32[64,128]{1,0:T(8,128)S(1)}, u32[]{:S(2)}, u32[]{:S(2)}) collective-permute-start(f32[64,128]{1,0:T(8,128)S(1)} %get-tuple-element.19), channel_id=1, source_target_pairs={{0,2},{2,0},{4,6},{6,4},{8,10},{10,8},{12,14},{14,12},{1,3},{3,1},... | collective-permute-start | bytes 98312 | tf_op jit(solution)/shard_map/ppermute | solution.py:158
  28.6 2.3 %collective-permute-start.5 = (f32[64,128]{1,0:T(8,128)S(1)}, f32[64,128]{1,0:T(8,128)S(1)}, u32[]{:S(2)}, u32[]{:S(2)}) collective-permute-start(f32[64,128]{1,0:T(8,128)S(1)} %get-tuple-element.20), channel_id=1, source_target_pairs={{0,4},{2,6},{4,0},{6,2},{8,12},{10,14},{12,8},{14,10},{1,5},{3,7},... | collective-permute-start | bytes 98312 | tf_op jit(solution)/shard_map/ppermute | solution.py:158
  30.9 0.0 collective-permute-done.1
  30.9 0.0 collective-permute-done.2
  30.9 0.0 collective-permute-done
  30.9 5.4 %collective-permute-start.3 = (f32[64,128]{1,0:T(8,128)S(1)}, f32[64,128]{1,0:T(8,128)S(1)}, u32[]{:S(2)}, u32[]{:S(2)}) collective-permute-start(f32[64,128]{1,0:T(8,128)S(1)} %fusion.2), channel_id=1, source_target_pairs={{0,12},{2,14},{4,8},{6,10},{8,4},{10,6},{12,0},{14,2},{1,13},{3,15... | collective-permute-start | bytes 98312 | tf_op jit(solution)/shard_map/ppermute | solution.py:158
  36.3 0.0 copy-start
  36.3 0.0 copy-start.1
  36.3 0.0 copy-start.2
  36.3 2.0 %copy.12 = f32[1,1,8192,128]{3,2,1,0:T(8,128)} copy(f32[1,1,8192,128]{3,2,1,0:T(8,128)S(1)} %get-tuple-element.28) | data formatting | bytes 8388608
  38.3 0.0 collective-permute-done.4
  38.3 0.0 collective-permute-done.5
  38.3 0.0 collective-permute-done.3
  38.3 0.0 copy-done
  38.3 0.0 copy-done.1
  38.3 0.0 copy-done.2
  38.4 0.7 %multiply_subtract_fusion = (f32[64,128]{1,0:T(8,128)}, f32[64,128]{1,0:T(8,128)}, f32[64,128]{1,0:T(8,128)}) fusion(f32[64,128]{1,0:T(8,128)S(1)} %copy-done, f32[64,128]{1,0:T(8,128)S(1)} %copy-done.1, f32[64,128]{1,0:T(8,128)S(1)} %copy-done.2, f32[64,128]{1,0:T(8,128)S(1)} %collective-permute-done.5, f32[64,128]{1,0:T(8,128)S(1)} %collective-permute-done.4, ...), kind=kLoop, calls=%fused_computation.9 | loop fusion | flops 139264 | bytes 360448 | tf_op jit(solution)/shard_map/sub | solution.py:176
  (1 shorter events, 0.0 us)
Async XLA Ops:
  23.1 7.8 %collective-permute-start = (f32[128,128]{1,0:T(8,128)S(1)}, f32[128,128]{1,0:T(8,128)S(1)}, u32[]{:S(2)}, u32[]{:S(2)}) collective-permute-start(f32[128,128]{1,0:T(8,128)S(1)} %get-tuple-element.15), channel_id=1, source_target_pairs={{0,6},{2,4},{4,2},{6,0},{8,14},{10,12},{12,10},{14,8},{1,7},{3,5},... | collective-permute-start | bytes 196616 | tf_op jit(solution)/shard_map/ppermute | solution.py:158
  25.1 5.8 %collective-permute-start.1 = (f32[64,128]{1,0:T(8,128)S(1)}, f32[64,128]{1,0:T(8,128)S(1)}, u32[]{:S(2)}, u32[]{:S(2)}) collective-permute-start(f32[64,128]{1,0:T(8,128)S(1)} %get-tuple-element.17), channel_id=1, source_target_pairs={{0,4},{2,6},{4,0},{6,2},{8,12},{10,14},{12,8},{14,10},{1,5},{3,7},... | collective-permute-start | bytes 98312 | tf_op jit(solution)/shard_map/ppermute | solution.py:158
  26.6 4.3 %collective-permute-start.2 = (f32[64,128]{1,0:T(8,128)S(1)}, f32[64,128]{1,0:T(8,128)S(1)}, u32[]{:S(2)}, u32[]{:S(2)}) collective-permute-start(f32[64,128]{1,0:T(8,128)S(1)} %get-tuple-element.18), channel_id=1, source_target_pairs={{0,2},{2,0},{4,6},{6,4},{8,10},{10,8},{12,14},{14,12},{1,3},{3,1},... | collective-permute-start | bytes 98312 | tf_op jit(solution)/shard_map/ppermute | solution.py:158
  28.0 10.4 %collective-permute-start.4 = (f32[64,128]{1,0:T(8,128)S(1)}, f32[64,128]{1,0:T(8,128)S(1)}, u32[]{:S(2)}, u32[]{:S(2)}) collective-permute-start(f32[64,128]{1,0:T(8,128)S(1)} %get-tuple-element.19), channel_id=1, source_target_pairs={{0,2},{2,0},{4,6},{6,4},{8,10},{10,8},{12,14},{14,12},{1,3},{3,1},... | collective-permute-start | bytes 98312 | tf_op jit(solution)/shard_map/ppermute | solution.py:158
  28.6 9.7 %collective-permute-start.5 = (f32[64,128]{1,0:T(8,128)S(1)}, f32[64,128]{1,0:T(8,128)S(1)}, u32[]{:S(2)}, u32[]{:S(2)}) collective-permute-start(f32[64,128]{1,0:T(8,128)S(1)} %get-tuple-element.20), channel_id=1, source_target_pairs={{0,4},{2,6},{4,0},{6,2},{8,12},{10,14},{12,8},{14,10},{1,5},{3,7},... | collective-permute-start | bytes 98312 | tf_op jit(solution)/shard_map/ppermute | solution.py:158
  30.9 7.4 %collective-permute-start.3 = (f32[64,128]{1,0:T(8,128)S(1)}, f32[64,128]{1,0:T(8,128)S(1)}, u32[]{:S(2)}, u32[]{:S(2)}) collective-permute-start(f32[64,128]{1,0:T(8,128)S(1)} %fusion.2), channel_id=1, source_target_pairs={{0,12},{2,14},{4,8},{6,10},{8,4},{10,6},{12,0},{14,2},{1,13},{3,15... | collective-permute-start | bytes 98312 | tf_op jit(solution)/shard_map/ppermute | solution.py:158
  36.3 2.0 %copy-start = (f32[64,128]{1,0:T(8,128)S(1)}, f32[64,128]{1,0:T(8,128)}, u32[]{:S(2)}) copy-start(f32[64,128]{1,0:T(8,128)} %param.11) | copy-start | bytes 98308
  36.3 2.0 %copy-start.1 = (f32[64,128]{1,0:T(8,128)S(1)}, f32[64,128]{1,0:T(8,128)}, u32[]{:S(2)}) copy-start(f32[64,128]{1,0:T(8,128)} %param.13) | copy-start | bytes 98308
  36.3 2.0 %copy-start.2 = (f32[64,128]{1,0:T(8,128)S(1)}, f32[64,128]{1,0:T(8,128)}, u32[]{:S(2)}) copy-start(f32[64,128]{1,0:T(8,128)} %param.12) | copy-start | bytes 98308

commit v9 on v7

--- a/solution.py
+++ b/solution.py
@@ -128,9 +128,9 @@
         return one_hot(rows, jnp.where(ids < 0, -1, ids ^ (me * own_rows)))
 
     halves = jnp.zeros((rows, 2 * width), jnp.float32)
-    for pair in range(0, sources // 2, 2):
-        named = jnp.concatenate([hot(pair), hot(pair + 1)], axis=1)
-        parts = [split(tile(source)) for source in range(2 * pair, 2 * pair + 4)]
+    for pair in range(0, sources // 2, 4):
+        named = jnp.concatenate([hot(pair + more) for more in range(4)], axis=1)
+        parts = [split(tile(source)) for source in range(2 * pair, 2 * pair + 8)]
         halves += jnp.dot(named, jnp.concatenate(parts, axis=0), preferred_element_type=jnp.float32)
     total = halves[:, :width] + halves[:, width:]
     for group, ref in zip(blocks, sums):

time: 39.1 us -> 39.1 us (level)
  no operation moved by 1% of the time
where the time goes in v9:
time: 39.1 us; the launch traced here: 39 us
  blocking collectives  18.6 us (48%)
  starting transfers between devices  13.1 us (34%)
  Pallas kernels  3.84 us (10%)
  local copies, waits for them, and re-layouts  2.02 us (5%)
  between operations  0.69 us (2%)
  other arithmetic  0.67 us (2%)
    all_to_all x1, blocking collectives, body(): lax.all_to_all(tiles.reshape(rows, 1, width), 'region', split_axis=0, con...  18.6 us
    ppermute x6, starting transfers between devices, swapped(): lax.ppermute(value, 'replica', [(source, source ^ mask) for source in ran...  13.1 us
    pallas_call x1, Pallas kernels, pack(): pl.pallas_call(functools.partial(pack_kernel, chunks), in_specs=[pl.Block...  3.4 us
    unnamed x7, local copies, waits for them, and re-layouts  2.02 us
  transfers between devices with their start and end apart: 6, of which 0 were waited for; matrix products, arithmetic and copies ran while one was open for 5% of the time, Pallas kernels for 0%

profile of v9, /device:TPU:32, one launch (start us, length us, event | category | flops | bytes accessed | tf_op | source)
XLA Modules:
  0.0 39.0 jit_solution(16158204644043863605)
XLA Ops:
  0.6 3.4 %pack.1 = (f32[1040,128]{1,0:T(8,128)S(1)}, f32[1,1,8192,128]{3,2,1,0:T(8,128)S(1)}) custom-call(s32[1,1,16]{2,1,0:T(1,128)} %counts_in.1, s32[1,1,16,64]{3,2,1,0:T(8,128)} %picked_in.1, bf16[1,1,8192,128]{3,2,1,0:T(8,128)(2,1)} %gradient.1, f32[1,1,8192,128]{3,2,1,0:T(8,128)} %feedback.1), custom_call_target="tpu_custom_call" | custom-call | tf_op jit(solution)/shard_map/pack/pallas_call | solution.py:92
  4.0 18.6 %all_to_all.5 = f32[1040,1,128]{2,1,0:T(1,128)S(1)} all-to-all(f32[1040,1,128]{2,1,0:T(1,128)S(1)} %bitcast.5), channel_id=1, replica_groups=mesh['region'=16,'replica'=8,'tensor'=2] {'region'}, dimensions={0} | all-to-all | bytes 1064960 | tf_op jit(solution)/shard_map/all_to_all | solution.py:163
  22.7 0.4 %gather_sum.1 = (f32[128,128]{1,0:T(8,128)S(1)}, f32[64,128]{1,0:T(8,128)S(1)}, f32[64,128]{1,0:T(8,128)S(1)}, f32[64,128]{1,0:T(8,128)S(1)}, f32[64,128]{1,0:T(...) custom-call(f32[1040,128]{1,0:T(8,128)S(1)} %bitcast.4), custom_call_target="tpu_custom_call" | custom-call | tf_op jit(solution)/shard_map/gather_sum/pallas_call | solution.py:144
  23.1 2.0 %collective-permute-start = (f32[128,128]{1,0:T(8,128)S(1)}, f32[128,128]{1,0:T(8,128)S(1)}, u32[]{:S(2)}, u32[]{:S(2)}) collective-permute-start(f32[128,128]{1,0:T(8,128)S(1)} %get-tuple-element.15), channel_id=1, source_target_pairs={{0,6},{2,4},{4,2},{6,0},{8,14},{10,12},{12,10},{14,8},{1,7},{3,5},... | collective-permute-start | bytes 196616 | tf_op jit(solution)/shard_map/ppermute | solution.py:155
  25.1 1.5 %collective-permute-start.1 = (f32[64,128]{1,0:T(8,128)S(1)}, f32[64,128]{1,0:T(8,128)S(1)}, u32[]{:S(2)}, u32[]{:S(2)}) collective-permute-start(f32[64,128]{1,0:T(8,128)S(1)} %get-tuple-element.17), channel_id=1, source_target_pairs={{0,4},{2,6},{4,0},{6,2},{8,12},{10,14},{12,8},{14,10},{1,5},{3,7},... | collective-permute-start | bytes 98312 | tf_op jit(solution)/shard_map/ppermute | solution.py:155
  26.6 1.4 %collective-permute-start.2 = (f32[64,128]{1,0:T(8,128)S(1)}, f32[64,128]{1,0:T(8,128)S(1)}, u32[]{:S(2)}, u32[]{:S(2)}) collective-permute-start(f32[64,128]{1,0:T(8,128)S(1)} %get-tuple-element.18), channel_id=1, source_target_pairs={{0,2},{2,0},{4,6},{6,4},{8,10},{10,8},{12,14},{14,12},{1,3},{3,1},... | collective-permute-start | bytes 98312 | tf_op jit(solution)/shard_map/ppermute | solution.py:155
  28.0 0.7 %collective-permute-start.4 = (f32[64,128]{1,0:T(8,128)S(1)}, f32[64,128]{1,0:T(8,128)S(1)}, u32[]{:S(2)}, u32[]{:S(2)}) collective-permute-start(f32[64,128]{1,0:T(8,128)S(1)} %get-tuple-element.19), channel_id=1, source_target_pairs={{0,2},{2,0},{4,6},{6,4},{8,10},{10,8},{12,14},{14,12},{1,3},{3,1},... | collective-permute-start | bytes 98312 | tf_op jit(solution)/shard_map/ppermute | solution.py:155
  28.6 2.3 %collective-permute-start.5 = (f32[64,128]{1,0:T(8,128)S(1)}, f32[64,128]{1,0:T(8,128)S(1)}, u32[]{:S(2)}, u32[]{:S(2)}) collective-permute-start(f32[64,128]{1,0:T(8,128)S(1)} %get-tuple-element.20), channel_id=1, source_target_pairs={{0,4},{2,6},{4,0},{6,2},{8,12},{10,14},{12,8},{14,10},{1,5},{3,7},... | collective-permute-start | bytes 98312 | tf_op jit(solution)/shard_map/ppermute | solution.py:155
  30.9 0.0 collective-permute-done.1
  30.9 0.0 collective-permute-done.2
  30.9 0.0 collective-permute-done
  30.9 5.4 %collective-permute-start.3 = (f32[64,128]{1,0:T(8,128)S(1)}, f32[64,128]{1,0:T(8,128)S(1)}, u32[]{:S(2)}, u32[]{:S(2)}) collective-permute-start(f32[64,128]{1,0:T(8,128)S(1)} %fusion.2), channel_id=1, source_target_pairs={{0,12},{2,14},{4,8},{6,10},{8,4},{10,6},{12,0},{14,2},{1,13},{3,15... | collective-permute-start | bytes 98312 | tf_op jit(solution)/shard_map/ppermute | solution.py:155
  36.3 0.0 copy-start
  36.3 0.0 copy-start.1
  36.3 0.0 copy-start.2
  36.3 2.0 %copy.12 = f32[1,1,8192,128]{3,2,1,0:T(8,128)} copy(f32[1,1,8192,128]{3,2,1,0:T(8,128)S(1)} %get-tuple-element.28) | data formatting | bytes 8388608
  38.3 0.0 collective-permute-done.4
  38.3 0.0 collective-permute-done.5
  38.3 0.0 collective-permute-done.3
  38.3 0.0 copy-done
  38.3 0.0 copy-done.1
  38.3 0.0 copy-done.2
  38.4 0.7 %multiply_subtract_fusion = (f32[64,128]{1,0:T(8,128)}, f32[64,128]{1,0:T(8,128)}, f32[64,128]{1,0:T(8,128)}) fusion(f32[64,128]{1,0:T(8,128)S(1)} %copy-done, f32[64,128]{1,0:T(8,128)S(1)} %copy-done.1, f32[64,128]{1,0:T(8,128)S(1)} %copy-done.2, f32[64,128]{1,0:T(8,128)S(1)} %collective-permute-done.5, f32[64,128]{1,0:T(8,128)S(1)} %collective-permute-done.4, ...), kind=kLoop, calls=%fused_computation.9 | loop fusion | flops 139264 | bytes 360448 | tf_op jit(solution)/shard_map/sub | solution.py:173
  (1 shorter events, 0.0 us)
Async XLA Ops:
  23.1 7.8 %collective-permute-start = (f32[128,128]{1,0:T(8,128)S(1)}, f32[128,128]{1,0:T(8,128)S(1)}, u32[]{:S(2)}, u32[]{:S(2)}) collective-permute-start(f32[128,128]{1,0:T(8,128)S(1)} %get-tuple-element.15), channel_id=1, source_target_pairs={{0,6},{2,4},{4,2},{6,0},{8,14},{10,12},{12,10},{14,8},{1,7},{3,5},... | collective-permute-start | bytes 196616 | tf_op jit(solution)/shard_map/ppermute | solution.py:155
  25.1 5.8 %collective-permute-start.1 = (f32[64,128]{1,0:T(8,128)S(1)}, f32[64,128]{1,0:T(8,128)S(1)}, u32[]{:S(2)}, u32[]{:S(2)}) collective-permute-start(f32[64,128]{1,0:T(8,128)S(1)} %get-tuple-element.17), channel_id=1, source_target_pairs={{0,4},{2,6},{4,0},{6,2},{8,12},{10,14},{12,8},{14,10},{1,5},{3,7},... | collective-permute-start | bytes 98312 | tf_op jit(solution)/shard_map/ppermute | solution.py:155
  26.6 4.3 %collective-permute-start.2 = (f32[64,128]{1,0:T(8,128)S(1)}, f32[64,128]{1,0:T(8,128)S(1)}, u32[]{:S(2)}, u32[]{:S(2)}) collective-permute-start(f32[64,128]{1,0:T(8,128)S(1)} %get-tuple-element.18), channel_id=1, source_target_pairs={{0,2},{2,0},{4,6},{6,4},{8,10},{10,8},{12,14},{14,12},{1,3},{3,1},... | collective-permute-start | bytes 98312 | tf_op jit(solution)/shard_map/ppermute | solution.py:155
  28.0 10.4 %collective-permute-start.4 = (f32[64,128]{1,0:T(8,128)S(1)}, f32[64,128]{1,0:T(8,128)S(1)}, u32[]{:S(2)}, u32[]{:S(2)}) collective-permute-start(f32[64,128]{1,0:T(8,128)S(1)} %get-tuple-element.19), channel_id=1, source_target_pairs={{0,2},{2,0},{4,6},{6,4},{8,10},{10,8},{12,14},{14,12},{1,3},{3,1},... | collective-permute-start | bytes 98312 | tf_op jit(solution)/shard_map/ppermute | solution.py:155
  28.6 9.7 %collective-permute-start.5 = (f32[64,128]{1,0:T(8,128)S(1)}, f32[64,128]{1,0:T(8,128)S(1)}, u32[]{:S(2)}, u32[]{:S(2)}) collective-permute-start(f32[64,128]{1,0:T(8,128)S(1)} %get-tuple-element.20), channel_id=1, source_target_pairs={{0,4},{2,6},{4,0},{6,2},{8,12},{10,14},{12,8},{14,10},{1,5},{3,7},... | collective-permute-start | bytes 98312 | tf_op jit(solution)/shard_map/ppermute | solution.py:155
  30.9 7.4 %collective-permute-start.3 = (f32[64,128]{1,0:T(8,128)S(1)}, f32[64,128]{1,0:T(8,128)S(1)}, u32[]{:S(2)}, u32[]{:S(2)}) collective-permute-start(f32[64,128]{1,0:T(8,128)S(1)} %fusion.2), channel_id=1, source_target_pairs={{0,12},{2,14},{4,8},{6,10},{8,4},{10,6},{12,0},{14,2},{1,13},{3,15... | collective-permute-start | bytes 98312 | tf_op jit(solution)/shard_map/ppermute | solution.py:155
  36.3 2.0 %copy-start = (f32[64,128]{1,0:T(8,128)S(1)}, f32[64,128]{1,0:T(8,128)}, u32[]{:S(2)}) copy-start(f32[64,128]{1,0:T(8,128)} %param.11) | copy-start | bytes 98308
  36.3 2.0 %copy-start.1 = (f32[64,128]{1,0:T(8,128)S(1)}, f32[64,128]{1,0:T(8,128)}, u32[]{:S(2)}) copy-start(f32[64,128]{1,0:T(8,128)} %param.13) | copy-start | bytes 98308
  36.3 2.0 %copy-start.2 = (f32[64,128]{1,0:T(8,128)S(1)}, f32[64,128]{1,0:T(8,128)}, u32[]{:S(2)}) copy-start(f32[64,128]{1,0:T(8,128)} %param.12) | copy-start | bytes 98308
